TPU v7x, 32 devices: a whole 2x2x4 slice. The times are simulated.
32 devices in a mesh: seq: 8 (over z, core), head: 4 (over y, x).
Axes of the slice: x: 2, y: 2, z: 4, core: 2. Of those that a mesh axis runs over, the one named last changes fastest.
Arguments:
- features: bfloat16 [8192, 8192], P(('seq', 'head')), may hold values from -6 to 6
- step_size: float32 [8192, 128], P(('seq', 'head')), may hold values from 0.01 to 0.08
- log_decay: float32 [8192, 128], P(('seq', 'head')), may hold values from -0.6 to 0
- inject: bfloat16 [8192, 1024], P(('seq', 'head')), may hold values from -1.5 to 1.5
- readout: bfloat16 [8192, 1024], P(('seq', 'head')), may hold values from -1.5 to 1.5
- skip_gain: float32 [128], replicated, may hold values from 0.5 to 1.5
Outputs:
- mixer_out: bfloat16 [8192, 8192], P(('seq', 'head'))
All inputs are finite; a program needn't handle non-finite values.
Results may differ from a plain program's by a relative error of at most 0.02.
Values may be sent and summed in bfloat16 or wider, within the bound.
A program may use at most 128 MiB of HBM per device.

v0:
```python
import jax
import jax.numpy as jnp
from jax import lax
from jax.sharding import PartitionSpec as P

HEAD_DIM = 64
STATE = 128
GROUPS = 8
SPAN = 512


def entering_2(x, axis, join, neutral):
    place = lax.axis_index(axis)
    gathered = jax.tree.map(
        lambda a, kind: lax.all_gather(a.astype(kind), axis), x, (jnp.bfloat16, jnp.bfloat16)
    )
    state = jax.tree.map(lambda a, e: jnp.zeros_like(a) + jnp.asarray(e, a.dtype), x, neutral)

    def one(step, state):
        return join(
            state,
            jax.tree.map(
                lambda a, own: lax.dynamic_index_in_dim(a, step, 0, False).astype(own.dtype),
                gathered,
                x,
            ),
        )

    return lax.fori_loop(0, place, one, state)


def shards(features, step_size, log_decay, inject, readout, skip_gain):
    head_ways = lax.axis_size("head")
    head_index = lax.axis_index("head")
    heads_all = step_size.shape[1]
    local_heads = heads_all // head_ways
    group_heads = heads_all // GROUPS
    local_groups = max(1, local_heads // group_heads)
    per_group = local_heads // local_groups
    regrouped = lax.all_to_all(features, "head", split_axis=1, concat_axis=0, tiled=True)
    steps_local, decay_local = (
        lax.all_to_all(
            step_size.astype(jnp.bfloat16), "head", split_axis=1, concat_axis=0, tiled=True
        ).astype(step_size.dtype),
        lax.all_to_all(
            log_decay.astype(jnp.bfloat16), "head", split_axis=1, concat_axis=0, tiled=True
        ).astype(log_decay.dtype),
    )
    inject_all, readout_all = (
        lax.all_gather(inject, "head", axis=0, tiled=True),
        lax.all_gather(readout, "head", axis=0, tiled=True),
    )
    first_col = head_index * local_heads // group_heads * STATE
    inject_mine = lax.dynamic_slice_in_dim(inject_all, first_col, local_groups * STATE, 1)
    readout_mine = lax.dynamic_slice_in_dim(readout_all, first_col, local_groups * STATE, 1)
    seq_rows = regrouped.shape[0]
    spans = seq_rows // SPAN
    drive = (
        regrouped.reshape(seq_rows, local_heads, HEAD_DIM).astype(jnp.float32)
        * steps_local[:, :, None]
    ).astype(jnp.bfloat16)
    drive_q = drive.reshape(spans, SPAN, local_groups, per_group, HEAD_DIM)
    cum_q = jnp.cumsum(decay_local.reshape(spans, SPAN, local_heads), axis=1)
    inject_q = inject_mine.reshape(spans, SPAN, local_groups, STATE)
    readout_q = readout_mine.reshape(spans, SPAN, local_groups, STATE)
    row_ids = lax.broadcasted_iota(jnp.int32, (SPAN, SPAN), 0)
    col_ids = lax.broadcasted_iota(jnp.int32, (SPAN, SPAN), 1)
    lower_mask = row_ids >= col_ids

    def span_terms(pieces):
        read_c, inject_c, drive_c, cum_c = pieces
        intersection = jnp.einsum(
            "ign,jgn->gij", read_c, inject_c, preferred_element_type=jnp.float32
        )
        cum_heads = cum_c.T
        log_gap = cum_heads[:, :, None] - cum_heads[:, None, :]
        decays = jnp.where(lower_mask, jnp.exp(jnp.where(lower_mask, log_gap, 0.0)), 0.0)
        weights = (
            decays.reshape(local_groups, per_group, SPAN, SPAN) * intersection[:, None]
        ).astype(jnp.bfloat16)
        inner_out = jnp.einsum(
            "ghij,jghp->ighp", weights, drive_c, preferred_element_type=jnp.float32
        )
        tail_decay = jnp.exp(cum_heads[:, -1:] - cum_heads)
        scaled = (
            drive_c.astype(jnp.float32)
            * tail_decay.T.reshape(SPAN, local_groups, per_group)[..., None]
        ).astype(jnp.bfloat16)
        summary = jnp.einsum("jghp,jgn->ghpn", scaled, inject_c, preferred_element_type=jnp.float32)
        return (inner_out, summary.reshape(local_heads, HEAD_DIM, STATE))

    inner_out, summary = lax.map(span_terms, (readout_q, inject_q, drive_q, cum_q))
    totals = cum_q[:, -1, :]

    def advance(carried, pieces):
        block_total, summary_c = pieces
        updated = carried * jnp.exp(block_total)[:, None, None] + summary_c
        return (updated, carried)

    zero_state = jnp.zeros((local_heads, HEAD_DIM, STATE), jnp.float32)
    end_state, entering = lax.scan(advance, zero_state, (totals, summary))
    dev_total = jnp.sum(totals, axis=0)

    def combine(earlier, following):
        return (
            earlier[0] + following[0],
            earlier[1] * jnp.exp(following[0])[:, None, None] + following[1],
        )

    identity = (jnp.zeros((local_heads,), jnp.float32), zero_state)
    scanned = entering_2((dev_total, end_state), "seq", combine, identity)
    incoming = scanned[1]
    before = jnp.cumsum(totals, axis=0) - totals
    states = entering + jnp.exp(before)[:, :, None, None] * incoming[None]
    held = states.astype(jnp.bfloat16).reshape(spans, local_groups, per_group, HEAD_DIM, STATE)
    outer_out = jnp.einsum("cign,cghpn->cighp", readout_q, held, preferred_element_type=jnp.float32)
    outer_out = outer_out * jnp.exp(cum_q).reshape(spans, SPAN, local_groups, per_group)[..., None]
    skip_local = lax.dynamic_slice_in_dim(skip_gain, head_index * local_heads, local_heads)
    plain = regrouped.reshape(spans, SPAN, local_groups, per_group, HEAD_DIM).astype(jnp.float32)
    total_out = (
        inner_out + outer_out + skip_local.reshape(local_groups, per_group)[:, :, None] * plain
    )
    mixed_rows = total_out.astype(jnp.bfloat16).reshape(seq_rows, local_heads * HEAD_DIM)
    return lax.all_to_all(mixed_rows, "head", split_axis=0, concat_axis=1, tiled=True)


def solution(mesh):
    placed = (
        P(("seq", "head"), None),
        P(("seq", "head"), None),
        P(("seq", "head"), None),
        P(("seq", "head"), None),
        P(("seq", "head"), None),
        P(),
    )
    return jax.shard_map(
        shards, mesh=mesh, in_specs=placed, out_specs=P(("seq", "head"), None), check_vma=False
    )
```

profile of v0, /device:TPU:0, one launch (start us, length us, event | category | flops | bytes accessed | tf_op | source)
XLA Modules:
  0.0 347.9 jit_solution(2939186529234307776)
XLA Ops:
  6.5 0.7 all-gather.6.cloned.1.call-update
  7.3 0.7 all-gather.8.cloned.1.call-update
  8.0 1.6 copy.44
  9.6 5.2 %all-to-all-start.2 = ((bf16[256,4,32]{0,2,1:T(8,128)(2,1)}), bf16[256,4,32]{0,2,1:T(8,128)(2,1)S(1)}, u32[]{:S(2)}, u32[]{:S(2)}) async-start(bf16[256,4,32]{0,2,1:T(8,128)(2,1)} %bitcast.6), calls=%async_computation.2 | async-start | bytes 131072 | tf_op jit(solution)/shard_map/all_to_all | solution.py:45
  14.8 1.6 copy.42
  16.4 3.2 all-to-all-done.2
  19.7 3.3 all-to-all-start.1
  22.9 6.4 %copy.40 = bf16[256,8192]{0,1:T(8,128)(2,1)} copy(bf16[256,8192]{1,0:T(8,128)(2,1)} %param.12) | data formatting | bytes 8388608 | tf_op args[0]
  29.3 4.8 %all-to-all-start = ((bf16[256,4,2048]{0,2,1:T(8,128)(2,1)}), bf16[256,4,2048]{0,2,1:T(8,128)(2,1)}, u32[]{:S(2)}, u32[]{:S(2)}) async-start(bf16[256,4,2048]{0,2,1:T(8,128)(2,1)} %bitcast.123), calls=%async_computation | async-start | bytes 8388608 | tf_op jit(solution)/shard_map/all_to_all | solution.py:40
  34.7 2.3 reduce-window.6
  37.6 0.6 copy-done.3
  38.2 0.8 slice_reduce_fusion.2
  39.0 42.5 %all-gather.6.cloned.1.call-done = bf16[1024,1024]{1,0:T(8,128)(2,1)} async-done(((bf16[256,1024]{1,0:T(8,128)(2,1)}), bf16[1024,1024]{1,0:T(8,128)(2,1)}) %all-gather.6.cloned.1.call-update) | async-done | bytes 2097168 | tf_op jit(solution)/shard_map/all_gather | solution.py:51
  81.6 1.1 constant_dynamic-slice_fusion.5
  82.6 0.9 reshape.115
  83.6 34.4 %all-gather.8.cloned.1.call-done = bf16[1024,1024]{1,0:T(8,128)(2,1)} async-done(((bf16[256,1024]{1,0:T(8,128)(2,1)}), bf16[1024,1024]{1,0:T(8,128)(2,1)}) %all-gather.8.cloned.1.call-update) | async-done | bytes 2097168 | tf_op jit(solution)/shard_map/all_gather | solution.py:50
  117.9 1.1 constant_dynamic-slice_fusion.4
  119.0 0.9 reshape.116
  119.9 2.9 convert_bitcast_fusion
  122.8 15.3 %copy.41 = f32[4,256,2048]{1,0,2:T(4,128)} copy(f32[4,256,2048]{1,2,0:T(8,128)S(1)} %convert_bitcast_fusion) | data formatting | bytes 16777216 | tf_op jit(solution)/shard_map/convert_element_type | solution.py:59
  138.2 11.9 %reshape.119 = f32[2,512,2,16,64]{1,0,4,3,2:T(2,128)} reshape(f32[4,256,2048]{1,0,2:T(4,128)} %copy.41) | data formatting | bytes 16777216 | tf_op jit(solution)/shard_map/convert_element_type | solution.py:59
  150.1 9.4 %multiply_convert_fusion.6 = bf16[2,512,2,16,64]{1,0,4,3,2:T(2,128)(2,1)} fusion(f32[2,512,2,16,64]{1,0,4,3,2:T(2,128)} %reshape.119, f32[2,512,2,16]{1,0,3,2:T(2,128)S(1)} %reshape.120), kind=kLoop, calls=%fused_computation.41 | loop fusion | flops 4194304 | bytes 12713984 | tf_op jit(solution)/shard_map/convert_element_type | solution.py:61
  159.5 5.1 %copy.49 = bf16[2,512,2,16,64]{1,4,3,2,0:T(8,128)(2,1)} copy(bf16[2,512,2,16,64]{1,0,4,3,2:T(2,128)(2,1)} %multiply_convert_fusion.6) | data formatting | bytes 8388608
  164.8 35.6 %while.40 = (s32[]{:T(128)}, f32[2,512,2,16,64]{1,4,3,2,0:T(8,128)}, f32[2,32,64,128]{3,2,1,0:T(8,128)S(1)}, bf16[2,512,2,16,64]{1,4,3,2,0:T(8,128)(2,1)}, f32[2...) while((s32[]{:T(128)}, ...), condition=%wide.region_3.4_spmd.clone.clone, body=%wide.region_2.3_spmd.clone.clone.sunk | while | flops 1521762304 | bytes 19204352 | solution.py:92
  165.0 1.5 constant_dynamic-slice_fusion.8
  167.0 0.9 constant_dynamic-slice_fusion.9
  167.9 12.0 %bitcast_dynamic-update-slice_fusion.6 = f32[2,512,2,16,64]{1,4,3,2,0:T(8,128)} fusion(f32[2,512,2,16,64]{1,4,3,2,0:T(8,128)} %get-tuple-element.367, s32[]{:T(128)} %get-tuple-element.366, f32[2,512,512]{2,1,0:T(8,128)S(1)} %fusion.37, f32[2,16,512]{2,1,0:T(8,128)S(1)} %bitcast.126, pred[512,512]{1,0:T(8,128)(4,1)S(1)} %iota_compare_fusion.2, ...), kind=kOutput, calls=%fused_computation.11.clone.1 | convolution fusion | flops 1115684864 | bytes 8782848 | tf_op jit(solution)/shard_map/while/body/eval_jaxpr/ghij,jghp->ighp/dot_general | solution.py:81
  180.3 2.3 fusion.39
  182.8 1.4 constant_dynamic-slice_fusion.8
  184.2 0.4 fusion.37
  184.6 0.9 constant_dynamic-slice_fusion.9
  185.6 12.1 %bitcast_dynamic-update-slice_fusion.6 = f32[2,512,2,16,64]{1,4,3,2,0:T(8,128)} fusion(f32[2,512,2,16,64]{1,4,3,2,0:T(8,128)} %get-tuple-element.367, s32[]{:T(128)} %get-tuple-element.366, f32[2,512,512]{2,1,0:T(8,128)S(1)} %fusion.37, f32[2,16,512]{2,1,0:T(8,128)S(1)} %bitcast.126, pred[512,512]{1,0:T(8,128)(4,1)S(1)} %iota_compare_fusion.2, ...), kind=kOutput, calls=%fused_computation.11.clone.1 | convolution fusion | flops 1115684864 | bytes 8782848 | tf_op jit(solution)/shard_map/while/body/eval_jaxpr/ghij,jghp->ighp/dot_general | solution.py:81
  198.0 2.3 fusion.39
  200.4 1.6 broadcast.20
  202.1 2.5 while.41
  202.1 1.0 bitcast_dynamic-update-slice_fusion.8
  203.4 1.0 bitcast_dynamic-update-slice_fusion.8
  204.6 0.9 convert_element_type.102
  205.7 0.6 dynamic-slice
  207.2 16.8 %all-reduce = bf16[256]{0:T(256)(128)(2,1)S(1)} all-reduce(bf16[256]{0:T(256)(128)(2,1)S(1)} %dynamic-update-slice), channel_id=2, replica_groups=mesh['seq'=8,'head'=4] {'seq'}, use_global_device_ids=true, to_apply=%add | all-reduce | flops 256 | bytes 1024
  224.3 28.7 %all-gather.10.cloned.1.call-done = bf16[256,64,128]{2,1,0:T(8,128)(2,1)} async-done(((bf16[32,64,128]{2,1,0:T(8,128)(2,1)}), bf16[256,64,128]{2,1,0:T(8,128)(2,1)}) %all-gather.10.cloned.1.call-update) | async-done | bytes 4194320 | tf_op jit(solution)/shard_map/all_gather | solution.py:15
  253.1 1.6 copy-done.2
  255.0 7.6 %fusion.22 = bf16[2,512,2,16,64]{1,4,3,2,0:T(8,128)(2,1)S(1)} fusion(f32[2,512,2,16,64]{1,4,3,2,0:T(8,128)} %get-tuple-element.123, f32[2,512,2,16,64]{1,0,4,3,2:T(2,128)} %reshape.119, f32[2,16]{1,0:T(2,128)S(1)} %mul.95, f32[2,512,2,16]{1,3,2,0:T(8,128)S(1)} %bitcast.130, bf16[2,2,16,64,128]{4,3,2,1,0:T(8,128)(2,1)S(1)} %bitcast.128, ...), kind=kOutput, calls=%fused_computation.38 | convolution fusion | flops 547356672 | bytes 22675584 | tf_op jit(solution)/shard_map/cign,cghpn->cighp/dot_general | solution.py:116
  262.7 6.4 %copy.54 = bf16[2,512,2,16,64]{1,0,4,3,2:T(2,128)(2,1)} copy(bf16[2,512,2,16,64]{1,4,3,2,0:T(8,128)(2,1)S(1)} %fusion.22) | data formatting | bytes 8388608 | tf_op jit(solution)/shard_map/convert_element_type | solution.py:123
  269.0 10.8 %all_to_all.50 = bf16[4,256,2048]{1,0,2:T(4,128)(2,1)} reshape(bf16[2,512,2,16,64]{1,0,4,3,2:T(2,128)(2,1)} %copy.54) | data formatting | bytes 8388608 | tf_op jit(solution)/shard_map/all_to_all | solution.py:124
  279.9 2.7 copy.55
  282.6 52.5 %all_to_all.58 = bf16[4,256,2048]{1,2,0:T(8,128)(2,1)} all-to-all(bf16[4,256,2048]{1,2,0:T(8,128)(2,1)S(1)} %copy.55), channel_id=1, replica_groups=mesh['seq'=8,'head'=4] {'head'}, dimensions={0} | all-to-all | bytes 8388608 | tf_op jit(solution)/shard_map/all_to_all | solution.py:124
  335.1 6.3 %copy.56 = bf16[256,8192]{1,0:T(8,128)(2,1)} copy(bf16[256,8192]{0,1:T(8,128)(2,1)} %bitcast.124) | data formatting | bytes 8388608 | tf_op jit(solution)/shard_map/all_to_all | solution.py:124
  (75 shorter events, 4.3 us)
Async XLA Ops:
  6.5 75.0 %all-gather.6.cloned.1.call-start = ((), (), s32[]{:S(2)}) async-start(), calls=%async_computation.4 | async-start | bytes 2621440 | tf_op jit(solution)/shard_map/all_gather | solution.py:51
  7.3 110.7 %all-gather.8.cloned.1.call-start = ((), (), s32[]{:S(2)}) async-start(), calls=%async_computation.5 | async-start | bytes 2621440 | tf_op jit(solution)/shard_map/all_gather | solution.py:50
  9.6 10.0 %all-to-all-start.2 = ((bf16[256,4,32]{0,2,1:T(8,128)(2,1)}), bf16[256,4,32]{0,2,1:T(8,128)(2,1)S(1)}, u32[]{:S(2)}, u32[]{:S(2)}) async-start(bf16[256,4,32]{0,2,1:T(8,128)(2,1)} %bitcast.6), calls=%async_computation.2 | async-start | bytes 131072 | tf_op jit(solution)/shard_map/all_to_all | solution.py:45
  19.7 9.7 %all-to-all-start.1 = ((bf16[256,4,32]{0,2,1:T(8,128)(2,1)}), bf16[256,4,32]{0,2,1:T(8,128)(2,1)S(1)}, u32[]{:S(2)}, u32[]{:S(2)}) async-start(bf16[256,4,32]{0,2,1:T(8,128)(2,1)} %bitcast.4), calls=%async_computation.1 | async-start | bytes 131072 | tf_op jit(solution)/shard_map/all_to_all | solution.py:42
  29.3 90.6 %all-to-all-start = ((bf16[256,4,2048]{0,2,1:T(8,128)(2,1)}), bf16[256,4,2048]{0,2,1:T(8,128)(2,1)}, u32[]{:S(2)}, u32[]{:S(2)}) async-start(bf16[256,4,2048]{0,2,1:T(8,128)(2,1)} %bitcast.123), calls=%async_computation | async-start | bytes 8388608 | tf_op jit(solution)/shard_map/all_to_all | solution.py:40
  34.2 218.8 %all-gather.10.cloned.1.call-start = ((), (), s32[]{:S(2)}) async-start(), calls=%async_computation.6 | async-start | bytes 4718592 | tf_op jit(solution)/shard_map/all_gather | solution.py:15
  37.0 2.0 copy-start.5
  37.2 1.8 copy-start.7
  37.6 0.7 copy-start.3
  164.8 37.2 %copy-start = (f32[32,64,128]{2,1,0:T(8,128)S(1)}, f32[32,64,128]{2,1,0:T(8,128)}, u32[]{:S(2)}) copy-start(f32[32,64,128]{2,1,0:T(8,128)} %custom-call) | copy-start | bytes 3145732
  164.8 37.2 %copy-start.9 = (f32[2,32]{1,0:T(2,128)S(1)}, f32[2,32]{1,0:T(2,128)}, u32[]{:S(2)}) copy-start(f32[2,32]{1,0:T(2,128)} %get-tuple-element.385) | copy-start | bytes 772
  167.9 12.0 %copy-start.4 = (f32[2,512,32]{1,2,0:T(8,128)S(1)}, f32[2,512,32]{1,2,0:T(8,128)}, u32[]{:S(2)}) copy-start(f32[2,512,32]{1,2,0:T(8,128)} %get-tuple-element.378) | copy-start | bytes 393220 | tf_op jit(solution)/shard_map/while
  185.6 12.1 %copy-start.4 = (f32[2,512,32]{1,2,0:T(8,128)S(1)}, f32[2,512,32]{1,2,0:T(8,128)}, u32[]{:S(2)}) copy-start(f32[2,512,32]{1,2,0:T(8,128)} %get-tuple-element.378) | copy-start | bytes 393220 | tf_op jit(solution)/shard_map/while
  202.0 3.5 %copy-start.11 = (f32[128]{0:T(128)S(1)}, f32[128]{0:T(128)}, u32[]{:S(2)}) copy-start(f32[128]{0:T(128)} %param.17) | copy-start | bytes 1540
  202.0 3.7 %copy-start.12 = (u32[32]{0:T(128)S(1)}, u32[32]{0:T(128)}, u32[]{:S(2)}) copy-start(u32[32]{0:T(128)} %constant.89) | copy-start | bytes 388
  202.0 4.9 %copy-start.10 = (bf16[32]{0:T(256)(128)(2,1)S(1)}, bf16[32]{0:T(256)(128)(2,1)}, u32[]{:S(2)}) copy-start(bf16[32]{0:T(256)(128)(2,1)} %get-tuple-element.210) | copy-start | bytes 196
  202.1 22.1 %copy-start.6 = (f32[2,32,4,128]{3,1,2,0:T(8,128)S(1)}, f32[2,32,4,128]{3,1,2,0:T(8,128)}, u32[]{:S(2)}) copy-start(f32[2,32,4,128]{3,1,2,0:T(8,128)} %copy-done.5) | copy-start | bytes 393220
  202.1 22.1 %copy-start.8 = (f32[2,32,4]{1,2,0:T(4,128)S(1)}, f32[2,32,4]{1,2,0:T(4,128)}, u32[]{:S(2)}) copy-start(f32[2,32,4]{1,2,0:T(4,128)} %copy-done.7) | copy-start | bytes 3076
  253.1 1.6 copy-start.2
  253.1 1.9 copy-start.1
Sparse Core Ops, SparseCore 0:
  9.2 72.3 all-gather.5
  83.4 34.4 all-gather.7
  205.7 47.2 all-gather.9
where the time goes:
time: 354 us; the launch traced here: 348 us
  waiting for transfers between devices  110 us (31%)
  local copies, waits for them, and re-layouts  83.6 us (24%)
  blocking collectives  69.2 us (20%)
  matrix products  37.2 us (11%)
  other arithmetic  19.8 us (6%)
  between operations  14.1 us (4%)
  starting transfers between devices  13.4 us (4%)
    all_to_all x1, blocking collectives, shards(): lax.all_to_all(mixed_rows, 'head', split_axis=0, concat_axis=1, tiled=True)  52.5 us
    all_gather x1, waiting for transfers between devices, shards(): lax.all_gather(readout, 'head', axis=0, tiled=True)  42.5 us
    all_gather x1, waiting for transfers between devices, shards(): lax.all_gather(inject, 'head', axis=0, tiled=True)  34.4 us
    all_gather x1, waiting for transfers between devices, entering_2(): lax.all_gather(a.astype(kind), axis)  28.7 us
    convert_element_type x2, local copies, waits for them, and re-layouts, shards(): regrouped.reshape(seq_rows, local_heads, HEAD_DIM).astype(jnp.float32)  27.2 us
    dot_general x2, matrix products, span_terms(): jnp.einsum('ghij,jghp->ighp', weights, drive_c, preferred_element_type=jn...  24.1 us
    all_to_all x3, local copies, waits for them, and re-layouts, shards(): lax.all_to_all(mixed_rows, 'head', split_axis=0, concat_axis=1, tiled=True)  19.9 us
    unnamed x31, local copies, waits for them, and re-layouts  17.8 us
  transfers between devices with their start and end apart: 6, of which 4 were waited for; matrix products, arithmetic and copies ran while one was open for 5% of the time, Pallas kernels for 0%

commit v1 on v0

v1 whole, which is shorter than its diff:
```python
import functools

import jax
import jax.numpy as jnp
from jax import lax
from jax.experimental import pallas as pl
from jax.experimental.pallas import tpu as pltpu
from jax.sharding import PartitionSpec as P

HEAD_DIM = 64
STATE = 128
GROUPS = 8
CHUNK = 128
F32 = jnp.float32
BF16 = jnp.bfloat16


def dot(a, b):
    return jnp.dot(a, b, preferred_element_type=F32)


def dot_rows(a, b):
    return lax.dot_general(a, b, (((0,), (0,)), ((), ())), preferred_element_type=F32)


def dot_last(a, b):
    return lax.dot_general(a, b, (((1,), (1,)), ((), ())), preferred_element_type=F32)


def lower(size):
    return lax.broadcasted_iota(jnp.int32, (size, size), 0) >= lax.broadcasted_iota(
        jnp.int32, (size, size), 1
    )


def cumulative(decay):
    ones = jnp.where(lower(CHUNK), 1.0, 0.0).astype(BF16)
    high = decay.astype(BF16)
    rest = decay - high.astype(F32)
    mid = rest.astype(BF16)
    low = (rest - mid.astype(F32)).astype(BF16)
    return dot(ones, high) + dot(ones, mid) + dot(ones, low)


def split(x):
    high = x.astype(BF16)
    return jnp.concatenate([high, (x - high.astype(F32)).astype(BF16)], axis=1)


def spread(group, heads, columns):
    head = lax.broadcasted_iota(jnp.int32, (2 * heads, columns), 0)
    head = jnp.where(head >= heads, head - heads, head)
    column = lax.broadcasted_iota(jnp.int32, (2 * heads, columns), 1)
    first = (head - group * (columns // HEAD_DIM)) * HEAD_DIM
    return jnp.where((column >= first) & (column < first + HEAD_DIM), 1.0, 0.0).astype(BF16)


def factors(step_ref, decay_ref):
    half = CHUNK // 2 - 1
    out = []
    for c in range(2):
        rows = pl.ds(c * CHUNK, CHUNK)
        cum = cumulative(decay_ref[rows, :])
        mid, end = cum[half : half + 1], cum[CHUNK - 1 : CHUNK]
        out.append((step_ref[rows, :] * jnp.exp(mid - cum), jnp.exp(cum - mid), mid, end))
    return out


def pad8(rows):
    rows = list(rows)
    return jnp.concatenate(rows + [jnp.zeros_like(rows[0])] * (16 - len(rows)), axis=0)


def summary_kernel(x_ref, step_ref, decay_ref, inject_ref, state_ref, total_ref, fac):
    heads = step_ref.shape[1]
    group = pl.program_id(0)

    @pl.when(group == 0)
    def _():
        (u0, _, m0, e0), (u1, _, m1, e1) = factors(step_ref, decay_ref)
        fac[...] = split(
            jnp.concatenate([u0, u1, pad8([jnp.exp(e0 - m0 + e1), jnp.exp(e1 - m1)])], axis=0)
        )
        total_ref[...] = e0 + e1

    wide = dot(fac[...], spread(group, heads, x_ref.shape[1]))
    state = None
    for c in range(2):
        rows = slice(c * CHUNK, (c + 1) * CHUNK)
        drive = (wide[rows] * x_ref[rows, :].astype(F32)).astype(BF16)
        part = dot_rows(inject_ref[rows, :], drive) * wide[2 * CHUNK + c : 2 * CHUNK + c + 1]
        state = part if state is None else state + part
    state_ref[...] = state.astype(BF16)


def output_kernel(
    x_ref, step_ref, decay_ref, inject_ref, readout_ref, skip_ref, held_ref, out_ref, fac
):
    heads = step_ref.shape[1]
    group = pl.program_id(0)

    @pl.when(group == 0)
    def _():
        (u0, w0, m0, e0), (u1, w1, m1, e1) = factors(step_ref, decay_ref)
        aux = [jnp.exp(m0), jnp.exp(m1 + e0), jnp.exp(m1 + e0 - m0), skip_ref[...]]
        fac[...] = split(jnp.concatenate([u0, u1, w0, w1, pad8(aux)], axis=0))

    wide = dot(fac[...], spread(group, heads, x_ref.shape[1]))
    aux = 4 * CHUNK
    held = held_ref[...].astype(F32)
    mask = lower(CHUNK)
    enter = held * wide[aux : aux + 1]
    for c in range(2):
        rows = slice(c * CHUNK, (c + 1) * CHUNK)
        x = x_ref[rows, :].astype(F32)
        drive = (wide[rows] * x).astype(BF16)
        inject, readout = inject_ref[rows, :], readout_ref[rows, :]
        cross = jnp.where(mask, dot_last(readout, inject), 0.0).astype(BF16)
        left = jnp.concatenate([cross, readout], axis=1)
        right = jnp.concatenate([drive, enter.astype(BF16)], axis=0)
        acc = dot(left, right)
        after = wide[(2 + c) * CHUNK : (3 + c) * CHUNK]
        out_ref[rows, :] = (after * acc + wide[aux + 3 : aux + 4] * x).astype(BF16)
        if c == 0:
            enter = held * wide[aux + 1 : aux + 2] + dot_rows(inject, drive) * wide[aux + 2 : aux + 3]


def shards(features, step_size, log_decay, inject, readout, skip_gain):
    ways, place = lax.axis_size("head"), lax.axis_index("head")
    seq_place, seq_ways = lax.axis_index("seq"), lax.axis_size("seq")
    tokens, width = features.shape
    heads = step_size.shape[1]
    block = width // GROUPS
    params = pltpu.CompilerParams(vmem_limit_bytes=48 * 2**20)
    wide_spec = pl.BlockSpec((tokens, block), lambda g: (0, g))
    full = pl.BlockSpec((tokens, heads), lambda g: (0, 0))
    group_spec = pl.BlockSpec((tokens, STATE), lambda g: (0, g))
    state_spec = pl.BlockSpec((STATE, block), lambda g: (0, g))
    row_spec = pl.BlockSpec((1, heads), lambda g: (0, 0))
    state, total = pl.pallas_call(
        summary_kernel,
        grid=(GROUPS,),
        in_specs=[wide_spec, full, full, group_spec],
        out_specs=[state_spec, row_spec],
        out_shape=[
            jax.ShapeDtypeStruct((STATE, width), BF16),
            jax.ShapeDtypeStruct((1, heads), F32),
        ],
        scratch_shapes=[pltpu.VMEM((2 * CHUNK + 16, 2 * heads), BF16)],
        compiler_params=params,
    )(features, step_size, log_decay, inject)

    totals = lax.all_gather(total[0], ("seq", "head")).reshape(seq_ways, ways, heads)
    own_heads = heads // ways
    mine = lax.dynamic_slice_in_dim(totals, place * own_heads, own_heads, 2)
    parts = lax.all_to_all(
        state.reshape(STATE, ways, width // ways), "head", split_axis=1, concat_axis=0, tiled=True
    ).reshape(ways, STATE, own_heads, HEAD_DIM).astype(F32)
    local = lax.dynamic_index_in_dim(mine, seq_place, 0, False)
    running = jnp.zeros(parts.shape[1:], F32)
    before, decays = [], []
    gone = jnp.zeros((own_heads,), F32)
    for j in range(ways):
        before.append(running)
        decays.append(gone)
        running = running * jnp.exp(local[j])[None, :, None] + parts[j]
        gone = gone + local[j]
    gathered = lax.all_gather(running.astype(BF16), "seq")
    seq_total = mine.sum(1)
    enter = jnp.zeros_like(running)
    for s in range(seq_ways):
        step = enter * jnp.exp(seq_total[s])[None, :, None] + gathered[s].astype(F32)
        enter = jnp.where(s < seq_place, step, enter)
    back = jnp.stack(
        [
            (enter * jnp.exp(decays[j])[None, :, None] + before[j]).astype(BF16)
            for j in range(ways)
        ]
    ).reshape(ways, STATE, width // ways)
    held = lax.all_to_all(back, "head", split_axis=0, concat_axis=2, tiled=True)[0]

    return pl.pallas_call(
        output_kernel,
        grid=(GROUPS,),
        in_specs=[wide_spec, full, full, group_spec, group_spec, row_spec, state_spec],
        out_specs=wide_spec,
        out_shape=jax.ShapeDtypeStruct((tokens, width), BF16),
        scratch_shapes=[pltpu.VMEM((4 * CHUNK + 16, 2 * heads), BF16)],
        compiler_params=params,
    )(features, step_size, log_decay, inject, readout, skip_gain[None], held)


def solution(mesh):
    rows = P(("seq", "head"), None)
    return jax.shard_map(
        shards,
        mesh=mesh,
        in_specs=(rows, rows, rows, rows, rows, P()),
        out_specs=rows,
        check_vma=False,
    )
```

time: 354 us -> 208 us (0.59); the launches traced: 348 us -> 208 us
  local copies, waits for them, and re-layouts: 83.6 us -> 8.66 us
  waiting for transfers between devices: 110 us -> 43.1 us
  blocking collectives: 69.2 us -> 113 us
  matrix products: 37.2 us -> 0 us
  Pallas kernels: 0 us -> 18.8 us
  other arithmetic: 19.8 us -> 5.57 us
  starting transfers between devices: 13.4 us -> 5.16 us
    all_gather x0 -> x1, blocking collectives: none -> 83.5 us  [shards(): lax.all_gather(total[0], ('seq', 'head')).reshape(seq_ways, ways, heads)]
    all_gather x3 -> x1, waiting for transfers between devices: 106 us -> 43 us  [shards(): gathered = lax.all_gather(running.astype(BF16), 'seq')]
    dot_general x7 -> x0, matrix products: 37.2 us -> none  [the longest x2 24.1 us: span_terms(): jnp.einsum('ghij,jghp->ighp', weights, drive_c, preferred_element_type=jn...]
    convert_element_type x5 -> x0, local copies, waits for them, and re-layouts: 33.8 us -> none  [the longest x2 27.2 us: shards(): regrouped.reshape(seq_rows, local_heads, HEAD_DIM).astype(jnp.float32)]
    all_to_all x1, blocking collectives: 52.5 us -> 29.3 us  [shards(): lax.all_to_all(back, 'head', split_axis=0, concat_axis=2, tiled=True)[0]]
    all_to_all x3 -> x0, local copies, waits for them, and re-layouts: 19.9 us -> none  [shards(): lax.all_to_all(mixed_rows, 'head', split_axis=0, concat_axis=1, tiled=True)]
    pallas_call x0 -> x2, Pallas kernels: none -> 18.8 us  [the longest x1 11.1 us: shards(): pl.pallas_call(output_kernel, grid=(GROUPS,), in_specs=[wide_spec, full,...]
    unnamed x1 -> x0, blocking collectives: 16.8 us -> none
  transfers between devices with their start and end apart: 6 -> 2, of which waited for: 4 -> 1; matrix products, arithmetic and copies ran while one was open for 5% -> 0% of each run, Pallas kernels for 0% -> 0%
where the time goes in v1:
time: 208 us
  blocking collectives  113 us (54%)
  waiting for transfers between devices  43.1 us (21%)
  Pallas kernels  18.8 us (9%)
  between operations  13.6 us (7%)
  local copies, waits for them, and re-layouts  8.66 us (4%)
  other arithmetic  5.57 us (3%)
  starting transfers between devices  5.16 us (2%)
    all_gather x1, blocking collectives, shards(): lax.all_gather(total[0], ('seq', 'head')).reshape(seq_ways, ways, heads)  83.5 us
    all_gather x1, waiting for transfers between devices, shards(): gathered = lax.all_gather(running.astype(BF16), 'seq')  43 us
    all_to_all x1, blocking collectives, shards(): lax.all_to_all(back, 'head', split_axis=0, concat_axis=2, tiled=True)[0]  29.3 us
    pallas_call x1, Pallas kernels, shards(): pl.pallas_call(output_kernel, grid=(GROUPS,), in_specs=[wide_spec, full,...  11.1 us
    pallas_call x1, Pallas kernels, shards(): pl.pallas_call(summary_kernel, grid=(GROUPS,), in_specs=[wide_spec, full,...  7.64 us
    all_to_all x1, starting transfers between devices, shards(): lax.all_to_all(state.reshape(STATE, ways, width // ways), 'head', split_a...  5.16 us
  transfers between devices with their start and end apart: 2, of which 1 were waited for; matrix products, arithmetic and copies ran while one was open for 0% of the time, Pallas kernels for 0%

profile of v1, /device:TPU:0, one launch (start us, length us, event | category | flops | bytes accessed | tf_op | source)
XLA Modules:
  0.0 207.7 jit_solution(2109286727329147054)
XLA Ops:
  6.5 0.0 copy-start
  6.5 1.0 copy-done
  7.6 0.0 copy-start.2
  7.6 0.9 copy-done.2
  8.5 0.0 copy-start.4
  8.5 0.9 copy-done.4
  9.4 7.6 %shard_map.64 = (bf16[128,8192]{1,0:T(8,128)(2,1)S(1)}, f32[1,128]{1,0:T(1,128)S(1)}) custom-call(bf16[256,8192]{1,0:T(8,128)(2,1)} %x_ref.3, f32[256,128]{1,0:T(8,128)S(1)} %copy-done.2, f32[256,128]{1,0:T(8,128)S(1)} %copy-done.4, bf16[256,1024]{1,0:T(8,128)(2,1)S(1)} %copy-done), custom_call_target="tpu_custom_call" | custom-call | tf_op jit(solution)/shard_map/pallas_call | solution.py:140
  17.0 2.4 %copy.11 = bf16[128,8192]{0,1:T(8,128)(2,1)} copy(bf16[128,8192]{1,0:T(8,128)(2,1)S(1)} %get-tuple-element.8) | data formatting | bytes 4194304 | tf_op jit(solution)/shard_map/reshape | solution.py:157
  19.5 5.2 %all-to-all-start = ((bf16[128,4,2048]{0,2,1:T(8,128)(2,1)}), bf16[128,4,2048]{0,2,1:T(8,128)(2,1)S(1)}, u32[]{:S(2)}, u32[]{:S(2)}) async-start(bf16[128,4,2048]{0,2,1:T(8,128)(2,1)} %bitcast.58), calls=%async_computation | async-start | bytes 4194304 | tf_op jit(solution)/shard_map/all_to_all | solution.py:156
  24.6 0.0 all-gather.3.cloned.1.call-start
  24.6 83.5 %all-gather = f32[32,1,128]{2,1,0:T(1,128)S(1)} all-gather(f32[1,1,128]{2,1,0:T(1,128)S(1)} %bitcast.53), channel_id=1, replica_groups=mesh['seq'=8,'head'=4] {'seq','head'}, dimensions={0}, use_global_device_ids=true | all-gather | bytes 16896 | tf_op jit(solution)/shard_map/all_gather | solution.py:153
  108.2 0.1 constant_dynamic-slice_fusion
  108.3 0.0 all-to-all-done
  108.3 0.3 convert_bitcast_fusion
  108.6 0.3 fusion.1
  108.9 1.2 add_convert_fusion.3
  110.1 0.0 all-gather.3.cloned.1.call-update
  110.1 0.1 dynamic-slice_reduce_fusion
  110.3 43.0 %all-gather.3.cloned.1.call-done = bf16[8,128,32,64]{1,3,2,0:T(8,128)(2,1)} async-done(((bf16[1,128,32,64]{1,3,2,0:T(8,128)(2,1)}), bf16[8,128,32,64]{1,3,2,0:T(8,128)(2,1)}) %all-gather.3.cloned.1.call-update) | async-done | bytes 4194320 | tf_op jit(solution)/shard_map/all_gather | solution.py:168
  153.3 3.1 %fusion = (bf16[1,128,32,64]{1,3,2,0:T(8,128)(2,1)S(1)}, f32[1,128,32,64]{1,3,2,0:T(8,128)S(1)}) fusion(bf16[8,128,32,64]{1,3,2,0:T(8,128)(2,1)} %all-gather.3.cloned.1.call-done, f32[32]{0:T(128)S(1)} %get-tuple-element.21, f32[32]{0:T(128)S(1)} %get-tuple-element.22, f32[32]{0:T(128)S(1)} %get-tuple-element.23, f32[32]{0:T(128)S(1)} %get-tuple-element.24, ...), kind=kLoop, calls=%fused_computation.27 | loop fusion | flops 8388608 | bytes 5768200 | tf_op jit(solution)/shard_map/convert_element_type | solution.py:176
  156.4 0.5 add_convert_fusion.1
  157.0 0.3 pad_maximum_fusion
  157.3 29.3 %all_to_all.24 = bf16[4,128,2048]{1,2,0:T(8,128)(2,1)} all-to-all(bf16[4,128,2048]{1,2,0:T(8,128)(2,1)S(1)} %pad_maximum_fusion), channel_id=1, replica_groups=mesh['seq'=8,'head'=4] {'head'}, dimensions={0} | all-to-all | bytes 4194304 | tf_op jit(solution)/shard_map/all_to_all | solution.py:180
  186.6 0.0 copy-start.1
  186.6 0.0 copy-start.3
  186.6 0.0 copy-start.5
  186.6 0.0 copy-start.6
  186.6 0.0 copy-start.7
  186.6 3.0 %copy.12.held_ref = bf16[128,8192]{1,0:T(8,128)(2,1)S(1)} copy(bf16[128,8192]{0,1:T(8,128)(2,1)} %bitcast.59) | data formatting | bytes 4194304 | tf_op jit(solution)/shard_map/squeeze | solution.py:180
  189.6 0.0 copy-done.1
  189.6 0.0 copy-done.3
  189.6 0.0 copy-done.5
  189.6 0.0 copy-done.6
  189.7 0.0 copy-done.7
  189.7 11.1 %shard_map.65 = bf16[256,8192]{1,0:T(8,128)(2,1)} custom-call(bf16[256,8192]{1,0:T(8,128)(2,1)} %x_ref.3, f32[256,128]{1,0:T(8,128)S(1)} %copy-done.3, f32[256,128]{1,0:T(8,128)S(1)} %copy-done.5, bf16[256,1024]{1,0:T(8,128)(2,1)S(1)} %copy-done.1, bf16[256,1024]{1,0:T(8,128)(2,1)S(1)} %copy-done.6, f32[1,128]{1,0:T(1,128)S(1)} %bitcast.52, ...), custom_call_target="tpu_custom_call" | custom-call | tf_op jit(solution)/shard_map/pallas_call | solution.py:182
  (3 shorter events, 0.0 us)
Async XLA Ops:
  6.5 1.0 copy-start
  7.6 0.9 copy-start.2
  8.5 0.9 copy-start.4
  19.5 88.8 %all-to-all-start = ((bf16[128,4,2048]{0,2,1:T(8,128)(2,1)}), bf16[128,4,2048]{0,2,1:T(8,128)(2,1)S(1)}, u32[]{:S(2)}, u32[]{:S(2)}) async-start(bf16[128,4,2048]{0,2,1:T(8,128)(2,1)} %bitcast.58), calls=%async_computation | async-start | bytes 4194304 | tf_op jit(solution)/shard_map/all_to_all | solution.py:156
  24.6 128.7 %all-gather.3.cloned.1.call-start = ((), (), s32[]{:S(2)}) async-start(), calls=%async_computation.2 | async-start | bytes 4718592 | tf_op jit(solution)/shard_map/all_gather | solution.py:168
  186.6 3.0 %copy-start.1 = (bf16[256,1024]{1,0:T(8,128)(2,1)S(1)}, bf16[256,1024]{1,0:T(8,128)(2,1)}, u32[]{:S(2)}) copy-start(bf16[256,1024]{1,0:T(8,128)(2,1)} %inject_ref.3) | copy-start | bytes 1572868
  186.6 3.0 %copy-start.3 = (f32[256,128]{1,0:T(8,128)S(1)}, f32[256,128]{1,0:T(8,128)}, u32[]{:S(2)}) copy-start(f32[256,128]{1,0:T(8,128)} %step_ref.3) | copy-start | bytes 393220
  186.6 3.1 %copy-start.5 = (f32[256,128]{1,0:T(8,128)S(1)}, f32[256,128]{1,0:T(8,128)}, u32[]{:S(2)}) copy-start(f32[256,128]{1,0:T(8,128)} %decay_ref.3) | copy-start | bytes 393220
  186.6 3.1 %copy-start.6 = (bf16[256,1024]{1,0:T(8,128)(2,1)S(1)}, bf16[256,1024]{1,0:T(8,128)(2,1)}, u32[]{:S(2)}) copy-start(bf16[256,1024]{1,0:T(8,128)(2,1)} %readout_ref.1) | copy-start | bytes 1572868
  186.6 3.1 %copy-start.7 = (f32[128]{0:T(128)S(1)}, f32[128]{0:T(128)}, u32[]{:S(2)}) copy-start(f32[128]{0:T(128)} %param.11) | copy-start | bytes 1540
Sparse Core Ops, SparseCore 0:
  110.2 43.0 all-gather.2

commit v2 on v1

--- a/solution.py
+++ b/solution.py
@@ -11,6 +11,8 @@
 STATE = 128
 GROUPS = 8
 CHUNK = 128
+PIECE = 512
+MESH = pl.DeviceIdType.MESH
 F32 = jnp.float32
 BF16 = jnp.bfloat16
 
@@ -71,26 +73,294 @@
     return jnp.concatenate(rows + [jnp.zeros_like(rows[0])] * (16 - len(rows)), axis=0)
 
 
-def summary_kernel(x_ref, step_ref, decay_ref, inject_ref, state_ref, total_ref, fac):
+def scan_kernel(
+    ways,
+    seqs,
+    x_ref,
+    step_ref,
+    decay_ref,
+    inject_ref,
+    held_ref,
+    fac,
+    tot,
+    pair,
+    dec,
+    up_stage,
+    parts,
+    down_stage,
+    total_stage,
+    total_in,
+    next_stage,
+    enter_in,
+    tot_send,
+    tot_recv,
+    pair_send,
+    pair_recv,
+    up_send,
+    up_recv,
+    down_send,
+    down_recv,
+    total_send,
+    total_recv,
+    next_send,
+    enter_recv,
+    keep_sem,
+):
     heads = step_ref.shape[1]
-    group = pl.program_id(0)
-
-    @pl.when(group == 0)
-    def _():
-        (u0, _, m0, e0), (u1, _, m1, e1) = factors(step_ref, decay_ref)
-        fac[...] = split(
-            jnp.concatenate([u0, u1, pad8([jnp.exp(e0 - m0 + e1), jnp.exp(e1 - m1)])], axis=0)
-        )
-        total_ref[...] = e0 + e1
-
-    wide = dot(fac[...], spread(group, heads, x_ref.shape[1]))
-    state = None
-    for c in range(2):
-        rows = slice(c * CHUNK, (c + 1) * CHUNK)
-        drive = (wide[rows] * x_ref[rows, :].astype(F32)).astype(BF16)
-        part = dot_rows(inject_ref[rows, :], drive) * wide[2 * CHUNK + c : 2 * CHUNK + c + 1]
-        state = part if state is None else state + part
-    state_ref[...] = state.astype(BF16)
+    width = x_ref.shape[1]
+    own = width // ways
+    depth = own // PIECE
+    me, seq = lax.axis_index("head"), lax.axis_index("seq")
+    core, chip = lax.rem(seq, 2), seq // 2
+    chips = seqs // 2
+    first = chip == 0
+
+    def peer(q):
+        return (seq, q)
+
+    def other(i):
+        return lax.rem(me + i, ways)
+
+    def remote(src, dst, send, recv, device):
+        return pltpu.make_async_remote_copy(
+            src_ref=src,
+            dst_ref=dst,
+            send_sem=send,
+            recv_sem=recv,
+            device_id=device,
+            device_id_type=MESH,
+        )
+
+    barrier = pltpu.get_barrier_semaphore()
+
+    def greet(device):
+        pl.semaphore_signal(barrier, inc=1, device_id=device, device_id_type=MESH)
+
+    for i in range(1, ways):
+        greet(peer(other(i)))
+
+    @pl.when(core == 1)
+    def _():
+        greet((seq - 1, me))
+
+    @pl.when((core == 1) & (chip > 0))
+    def _():
+        greet((seq - 2, me))
+
+    @pl.when((core == 0) & (chip > 0))
+    def _():
+        greet((seq - 1, me))
+
+    (u0, _, m0, e0), (u1, _, m1, e1) = factors(step_ref, decay_ref)
+    fac[...] = split(
+        jnp.concatenate([u0, u1, pad8([jnp.exp(e0 - m0 + e1), jnp.exp(e1 - m1)])], axis=0)
+    )
+    tot[me] = jnp.broadcast_to(e0 + e1, (8, heads))
+
+    @pl.when(first)
+    def _():
+        enter_in[...] = jnp.zeros_like(enter_in)
+
+    ahead = 2 - 2 * (chip // (chips - 1)) if chips > 1 else 0
+    pl.semaphore_wait(barrier, ways - core + core * ahead)
+
+    def tot_copy(q):
+        return remote(tot.at[me], tot.at[me], tot_send.at[q], tot_recv.at[me], peer(q))
+
+    def tot_from(q):
+        return remote(tot.at[q], tot.at[q], tot_send.at[q], tot_recv.at[q], peer(q))
+
+    def up_copy(k, q):
+        return remote(
+            up_stage.at[k, q], parts.at[k, me], up_send.at[k, q], up_recv.at[k, me], peer(q)
+        )
+
+    def up_from(k, q):
+        return remote(
+            up_stage.at[k, q], parts.at[k, q], up_send.at[k, q], up_recv.at[k, q], peer(q)
+        )
+
+    def down_copy(k, q):
+        return remote(
+            down_stage.at[k, q],
+            held_ref.at[me * depth + k],
+            down_send.at[k, q],
+            down_recv.at[k, me],
+            peer(q),
+        )
+
+    def down_from(k, q):
+        return remote(
+            down_stage.at[k, q],
+            held_ref.at[q * depth + k],
+            down_send.at[k, q],
+            down_recv.at[k, q],
+            peer(q),
+        )
+
+    def keep_copy(k):
+        return pltpu.make_async_copy(
+            down_stage.at[k, me], held_ref.at[me * depth + k], keep_sem.at[k]
+        )
+
+    def pair_copy():
+        return remote(pair.at[0], pair.at[1], pair_send, pair_recv, (seq + 1, me))
+
+    def total_copy(k):
+        return remote(
+            total_stage.at[k], total_in.at[k], total_send.at[k], total_recv.at[k], (seq + 1, me)
+        )
+
+    def next_copy(k, ahead):
+        return remote(
+            next_stage.at[k],
+            enter_in.at[k],
+            next_send.at[k, ahead - 1],
+            enter_recv.at[k],
+            (seq + ahead, me),
+        )
+
+    for i in range(1, ways):
+        tot_copy(other(i)).start()
+
+    def piece(t, carry):
+        k, i = t // ways, lax.rem(t, ways)
+        q = lax.rem(me + 1 + i, ways)
+        index = q * depth + k
+        columns = pl.ds(pl.multiple_of(index * PIECE, PIECE), PIECE)
+        group = index * PIECE // (width // GROUPS)
+        shared = pl.ds(pl.multiple_of(group * STATE, STATE), STATE)
+        wide = dot(fac[...], spread(index, heads, PIECE))
+        state = None
+        for c in range(2):
+            rows = slice(c * CHUNK, (c + 1) * CHUNK)
+            drive = (wide[rows] * x_ref[rows, columns].astype(F32)).astype(BF16)
+            part = dot_rows(inject_ref[rows, shared], drive)
+            part = part * wide[2 * CHUNK + c : 2 * CHUNK + c + 1]
+            state = part if state is None else state + part
+
+        @pl.when(i == ways - 1)
+        def _():
+            parts[k, me] = state.astype(BF16)
+
+        @pl.when(i < ways - 1)
+        def _():
+            up_stage[k, q] = state.astype(BF16)
+            up_copy(k, q).start()
+
+        return carry
+
+    lax.fori_loop(0, depth * ways, piece, 0)
+
+    for i in range(1, ways):
+        tot_from(other(i)).wait_recv()
+    logs = [tot[j][:1] for j in range(ways)]
+    whole = sum(logs[1:], logs[0])
+
+    @pl.when(core == 0)
+    def _():
+        pair[0] = jnp.broadcast_to(whole, (8, heads))
+        pair_copy().start()
+        pair[1] = jnp.zeros((8, heads), F32)
+
+    @pl.when(core == 1)
+    def _():
+        pair_copy().wait_recv()
+
+    rows = [jnp.exp(a) for a in logs] + [jnp.exp(pair[1][:1])]
+    rows = split(jnp.concatenate(rows + [jnp.zeros_like(rows[0])] * (-len(rows) % 16), axis=0))
+    for k in range(depth):
+        dec[k] = dot(rows, spread(me * depth + k, heads, PIECE))
+
+    def await_parts(k):
+        for i in range(1, ways):
+            up_from(k, other(i)).wait_recv()
+
+    def onward(k, running, j):
+        return running * dec[k, j : j + 1, :] + parts[k, j].astype(F32)
+
+    def returns(k, running):
+        for j in range(ways):
+            down_stage[k, j] = running.astype(BF16)
+            running = onward(k, running, j)
+        return running
+
+    def send_down(k):
+        for i in range(1, ways):
+            down_copy(k, other(i)).start()
+        keep_copy(k).start()
+
+    def await_enter(k):
+        @pl.when(chip > 0)
+        def _():
+            next_copy(k, 1).wait_recv()
+
+    @pl.when(core == 0)
+    def _():
+        def totals(k, carry):
+            await_parts(k)
+            running = parts[k, 0].astype(F32)
+            for j in range(1, ways):
+                running = onward(k, running, j)
+            total_stage[k] = running.astype(BF16)
+            total_copy(k).start()
+            return carry
+
+        def finish(k, carry):
+            await_enter(k)
+            returns(k, enter_in[k].astype(F32))
+            send_down(k)
+            return carry
+
+        lax.fori_loop(0, depth, totals, 0)
+        lax.fori_loop(0, depth, finish, 0)
+
+    @pl.when(core == 1)
+    def _():
+        def finish(k, carry):
+            await_parts(k)
+            total_copy(k).wait_recv()
+            await_enter(k)
+            start = enter_in[k].astype(F32) * dec[k, ways : ways + 1, :]
+            running = returns(k, start + total_in[k].astype(F32))
+
+            @pl.when(chip < chips - 1)
+            def _():
+                next_stage[k] = running.astype(BF16)
+                next_copy(k, 2).start()
+                next_copy(k, 1).start()
+
+            send_down(k)
+            return carry
+
+        lax.fori_loop(0, depth, finish, 0)
+
+    def drain(k, carry):
+        for i in range(1, ways):
+            down_from(k, other(i)).wait_recv()
+        for i in range(1, ways):
+            up_copy(k, other(i)).wait_send()
+            down_copy(k, other(i)).wait_send()
+        keep_copy(k).wait()
+
+        @pl.when(core == 0)
+        def _():
+            total_copy(k).wait_send()
+
+        @pl.when((core == 1) & (chip < chips - 1))
+        def _():
+            next_copy(k, 2).wait_send()
+            next_copy(k, 1).wait_send()
+
+        return carry
+
+    lax.fori_loop(0, depth, drain, 0)
+    for i in range(1, ways):
+        tot_copy(other(i)).wait_send()
+
+    @pl.when(core == 0)
+    def _():
+        pair_copy().wait_send()
 
 
 def output_kernel(
@@ -107,7 +377,7 @@
 
     wide = dot(fac[...], spread(group, heads, x_ref.shape[1]))
     aux = 4 * CHUNK
-    held = held_ref[...].astype(F32)
+    held = jnp.concatenate([held_ref[i] for i in range(held_ref.shape[0])], axis=1).astype(F32)
     mask = lower(CHUNK)
     enter = held * wide[aux : aux + 1]
     for c in range(2):
@@ -126,59 +396,55 @@
 
 
 def shards(features, step_size, log_decay, inject, readout, skip_gain):
-    ways, place = lax.axis_size("head"), lax.axis_index("head")
-    seq_place, seq_ways = lax.axis_index("seq"), lax.axis_size("seq")
+    ways, seqs = lax.axis_size("head"), lax.axis_size("seq")
     tokens, width = features.shape
     heads = step_size.shape[1]
     block = width // GROUPS
+    depth = width // ways // PIECE
     params = pltpu.CompilerParams(vmem_limit_bytes=48 * 2**20)
+    vmem = pl.BlockSpec(memory_space=pltpu.VMEM)
+    dma = pltpu.SemaphoreType.DMA
+    held = pl.pallas_call(
+        functools.partial(scan_kernel, ways, seqs),
+        in_specs=[vmem] * 4,
+        out_specs=pl.BlockSpec(memory_space=pl.ANY),
+        out_shape=jax.ShapeDtypeStruct((width // PIECE, STATE, PIECE), BF16),
+        scratch_shapes=[
+            pltpu.VMEM((2 * CHUNK + 16, 2 * heads), BF16),
+            pltpu.VMEM((ways, 8, heads), F32),
+            pltpu.VMEM((2, 8, heads), F32),
+            pltpu.VMEM((depth, (ways + 16) // 16 * 16, PIECE), F32),
+            pltpu.VMEM((depth, ways, STATE, PIECE), BF16),
+            pltpu.VMEM((depth, ways, STATE, PIECE), BF16),
+            pltpu.VMEM((depth, ways, STATE, PIECE), BF16),
+            pltpu.VMEM((depth, STATE, PIECE), BF16),
+            pltpu.VMEM((depth, STATE, PIECE), BF16),
+            pltpu.VMEM((depth, STATE, PIECE), BF16),
+            pltpu.VMEM((depth, STATE, PIECE), BF16),
+            dma((ways,)),
+            dma((ways,)),
+            dma,
+            dma,
+            dma((depth, ways)),
+            dma((depth, ways)),
+            dma((depth, ways)),
+            dma((depth, ways)),
+            dma((depth,)),
+            dma((depth,)),
+            dma((depth, 2)),
+            dma((depth,)),
+            dma((depth,)),
+        ],
+        compiler_params=pltpu.CompilerParams(
+            vmem_limit_bytes=48 * 2**20, collective_id=0, has_side_effects=True
+        ),
+    )(features, step_size, log_decay, inject)
+
     wide_spec = pl.BlockSpec((tokens, block), lambda g: (0, g))
     full = pl.BlockSpec((tokens, heads), lambda g: (0, 0))
     group_spec = pl.BlockSpec((tokens, STATE), lambda g: (0, g))
-    state_spec = pl.BlockSpec((STATE, block), lambda g: (0, g))
+    state_spec = pl.BlockSpec((block // PIECE, STATE, PIECE), lambda g: (g, 0, 0))
     row_spec = pl.BlockSpec((1, heads), lambda g: (0, 0))
-    state, total = pl.pallas_call(
-        summary_kernel,
-        grid=(GROUPS,),
-        in_specs=[wide_spec, full, full, group_spec],
-        out_specs=[state_spec, row_spec],
-        out_shape=[
-            jax.ShapeDtypeStruct((STATE, width), BF16),
-            jax.ShapeDtypeStruct((1, heads), F32),
-        ],
-        scratch_shapes=[pltpu.VMEM((2 * CHUNK + 16, 2 * heads), BF16)],
-        compiler_params=params,
-    )(features, step_size, log_decay, inject)
-
-    totals = lax.all_gather(total[0], ("seq", "head")).reshape(seq_ways, ways, heads)
-    own_heads = heads // ways
-    mine = lax.dynamic_slice_in_dim(totals, place * own_heads, own_heads, 2)
-    parts = lax.all_to_all(
-        state.reshape(STATE, ways, width // ways), "head", split_axis=1, concat_axis=0, tiled=True
-    ).reshape(ways, STATE, own_heads, HEAD_DIM).astype(F32)
-    local = lax.dynamic_index_in_dim(mine, seq_place, 0, False)
-    running = jnp.zeros(parts.shape[1:], F32)
-    before, decays = [], []
-    gone = jnp.zeros((own_heads,), F32)
-    for j in range(ways):
-        before.append(running)
-        decays.append(gone)
-        running = running * jnp.exp(local[j])[None, :, None] + parts[j]
-        gone = gone + local[j]
-    gathered = lax.all_gather(running.astype(BF16), "seq")
-    seq_total = mine.sum(1)
-    enter = jnp.zeros_like(running)
-    for s in range(seq_ways):
-        step = enter * jnp.exp(seq_total[s])[None, :, None] + gathered[s].astype(F32)
-        enter = jnp.where(s < seq_place, step, enter)
-    back = jnp.stack(
-        [
-            (enter * jnp.exp(decays[j])[None, :, None] + before[j]).astype(BF16)
-            for j in range(ways)
-        ]
-    ).reshape(ways, STATE, width // ways)
-    held = lax.all_to_all(back, "head", split_axis=0, concat_axis=2, tiled=True)[0]
-
     return pl.pallas_call(
         output_kernel,
         grid=(GROUPS,),

time: 208 us -> 69 us (0.33)
  blocking collectives: 113 us -> 0 us
  Pallas kernels: 18.8 us -> 65.7 us
  waiting for transfers between devices: 43.1 us -> 0 us
  between operations: 13.6 us -> 0.03 us
  local copies, waits for them, and re-layouts: 8.66 us -> 2.87 us
  other arithmetic: 5.57 us -> 0 us
  starting transfers between devices: 5.16 us -> 0 us
    all_gather x1 -> x0, blocking collectives: 83.5 us -> none  [shards(): lax.all_gather(total[0], ('seq', 'head')).reshape(seq_ways, ways, heads)]
    pallas_call x1, Pallas kernels: 7.64 us -> 54.6 us  [shards(): pl.pallas_call(functools.partial(scan_kernel, ways, seqs), in_specs=[vmem...]
    all_gather x1 -> x0, waiting for transfers between devices: 43 us -> none  [shards(): gathered = lax.all_gather(running.astype(BF16), 'seq')]
    all_to_all x1 -> x0, blocking collectives: 29.3 us -> none  [shards(): lax.all_to_all(back, 'head', split_axis=0, concat_axis=2, tiled=True)[0]]
    convert_element_type x4 -> x0, other arithmetic: 5.18 us -> none  [the longest x2 3.66 us: shards(): (enter * jnp.exp(decays[j])[None, :, None] + before[j]).astype(BF16)]
    all_to_all x1 -> x0, starting transfers between devices: 5.16 us -> none  [shards(): lax.all_to_all(state.reshape(STATE, ways, width // ways), 'head', split_a...]
    squeeze x1 -> x0, local copies, waits for them, and re-layouts: 3 us -> none  [shards(): lax.all_to_all(back, 'head', split_axis=0, concat_axis=2, tiled=True)[0]]
    reshape x1 -> x0, local copies, waits for them, and re-layouts: 2.44 us -> none  [shards(): state.reshape(STATE, ways, width // ways)]
  transfers between devices with their start and end apart: 2 -> 0, of which waited for: 1 -> 0; matrix products, arithmetic and copies ran while one was open for 0% -> 0% of each run, Pallas kernels for 0% -> 0%
where the time goes in v2:
time: 69 us; the launch traced here: 68.6 us
  Pallas kernels  65.7 us (95%)
  local copies, waits for them, and re-layouts  2.87 us (4%)
    pallas_call x1, Pallas kernels, shards(): pl.pallas_call(functools.partial(scan_kernel, ways, seqs), in_specs=[vmem...  54.6 us
    pallas_call x1, Pallas kernels, shards(): pl.pallas_call(output_kernel, grid=(GROUPS,), in_specs=[wide_spec, full,...  11.1 us
    unnamed x10, local copies, waits for them, and re-layouts  2.87 us

profile of v2, /device:TPU:0, one launch (start us, length us, event | category | flops | bytes accessed | tf_op | source)
XLA Modules:
  0.0 68.6 jit_solution(9280096736284489019)
XLA Ops:
  0.0 0.0 copy-start.4
  0.0 0.0 copy-start
  0.0 1.1 %copy-done = bf16[256,1024]{1,0:T(8,128)(2,1)S(1)} copy-done((bf16[256,1024]{1,0:T(8,128)(2,1)S(1)}, bf16[256,1024]{1,0:T(8,128)(2,1)}, u32[]{:S(2)}) %copy-start) | copy-done | bytes 524312
  1.1 0.0 copy-start.1
  1.1 0.9 %copy-done.1 = f32[256,128]{1,0:T(8,128)S(1)} copy-done((f32[256,128]{1,0:T(8,128)S(1)}, f32[256,128]{1,0:T(8,128)}, u32[]{:S(2)}) %copy-start.1) | copy-done | bytes 131096
  2.0 0.0 copy-start.2
  2.0 0.9 %copy-done.2 = f32[256,128]{1,0:T(8,128)S(1)} copy-done((f32[256,128]{1,0:T(8,128)S(1)}, f32[256,128]{1,0:T(8,128)}, u32[]{:S(2)}) %copy-start.2) | copy-done | bytes 131096
  2.9 0.0 copy-start.3
  2.9 54.6 %shard_map.64.held_ref = bf16[16,128,512]{2,1,0:T(8,128)(2,1)S(1)} custom-call(bf16[256,8192]{1,0:T(8,128)(2,1)} %x_ref.3, f32[256,128]{1,0:T(8,128)S(1)} %copy-done.1, f32[256,128]{1,0:T(8,128)S(1)} %copy-done.2, bf16[256,1024]{1,0:T(8,128)(2,1)S(1)} %copy-done), custom_call_target="tpu_custom_call" | custom-call | tf_op jit(solution)/shard_map/pallas_call | solution.py:407
  57.4 0.0 copy-done.4
  57.4 0.0 copy-done.3
  57.5 11.1 %shard_map.65 = bf16[256,8192]{1,0:T(8,128)(2,1)} custom-call(bf16[256,8192]{1,0:T(8,128)(2,1)} %x_ref.3, f32[256,128]{1,0:T(8,128)S(1)} %copy-done.1, f32[256,128]{1,0:T(8,128)S(1)} %copy-done.2, bf16[256,1024]{1,0:T(8,128)(2,1)S(1)} %copy-done, bf16[256,1024]{1,0:T(8,128)(2,1)S(1)} %copy-done.3, f32[1,128]{1,0:T(1,128)S(1)} %bitcast.1, ...), custom_call_target="tpu_custom_call" | custom-call | tf_op jit(solution)/shard_map/pallas_call | solution.py:448
Async XLA Ops:
  0.0 57.4 %copy-start.4 = (f32[128]{0:T(128)S(1)}, f32[128]{0:T(128)}, u32[]{:S(2)}) copy-start(f32[128]{0:T(128)} %param.11) | copy-start | bytes 1540
  0.0 1.1 %copy-start = (bf16[256,1024]{1,0:T(8,128)(2,1)S(1)}, bf16[256,1024]{1,0:T(8,128)(2,1)}, u32[]{:S(2)}) copy-start(bf16[256,1024]{1,0:T(8,128)(2,1)} %inject_ref.3) | copy-start | bytes 1572868
  1.1 0.9 %copy-start.1 = (f32[256,128]{1,0:T(8,128)S(1)}, f32[256,128]{1,0:T(8,128)}, u32[]{:S(2)}) copy-start(f32[256,128]{1,0:T(8,128)} %step_ref.3) | copy-start | bytes 393220
  2.0 0.9 %copy-start.2 = (f32[256,128]{1,0:T(8,128)S(1)}, f32[256,128]{1,0:T(8,128)}, u32[]{:S(2)}) copy-start(f32[256,128]{1,0:T(8,128)} %decay_ref.3) | copy-start | bytes 393220
  2.9 54.6 %copy-start.3 = (bf16[256,1024]{1,0:T(8,128)(2,1)S(1)}, bf16[256,1024]{1,0:T(8,128)(2,1)}, u32[]{:S(2)}) copy-start(bf16[256,1024]{1,0:T(8,128)(2,1)} %readout_ref.1) | copy-start | bytes 1572868

commit v3 on v2

--- a/solution.py
+++ b/solution.py
@@ -73,15 +73,28 @@
     return jnp.concatenate(rows + [jnp.zeros_like(rows[0])] * (16 - len(rows)), axis=0)
 
 
-def scan_kernel(
+def mixer_kernel(
     ways,
     seqs,
+    x_hbm,
+    step_hbm,
+    decay_hbm,
+    inject_hbm,
+    readout_hbm,
+    skip_ref,
+    out_hbm,
     x_ref,
     step_ref,
     decay_ref,
     inject_ref,
+    readout_ref,
     held_ref,
+    drive_ref,
+    first_state,
+    after_ref,
+    left_ref,
     fac,
+    fac_out,
     tot,
     pair,
     dec,
@@ -105,6 +118,9 @@
     next_send,
     enter_recv,
     keep_sem,
+    load_sem,
+    x_sem,
+    out_sem,
 ):
     heads = step_ref.shape[1]
     width = x_ref.shape[1]
@@ -131,6 +147,37 @@
             device_id_type=MESH,
         )
 
+    def load(i):
+        src = (decay_hbm, step_hbm, inject_hbm, readout_hbm)[i]
+        dst = (decay_ref, step_ref, inject_ref, readout_ref)[i]
+        return pltpu.make_async_copy(src, dst, load_sem.at[i])
+
+    def columns_of(index):
+        return pl.ds(pl.multiple_of(index * PIECE, PIECE), PIECE)
+
+    def load_x(index):
+        columns = columns_of(index)
+        return pltpu.make_async_copy(x_hbm.at[:, columns], x_ref.at[:, columns], x_sem.at[index])
+
+    def store(index):
+        columns = columns_of(index)
+        return pltpu.make_async_copy(
+            x_ref.at[:, columns], out_hbm.at[:, columns], out_sem.at[index]
+        )
+
+    def place(t):
+        return lax.rem(me + 1 + lax.rem(t, ways), ways) * depth + t // ways
+
+    for i in range(3):
+        load(i).start()
+
+    def begin(t, carry):
+        load_x(place(t)).start()
+        return carry
+
+    lax.fori_loop(0, depth * ways, begin, 0)
+    load(3).start()
+
     barrier = pltpu.get_barrier_semaphore()
 
     def greet(device):
@@ -151,10 +198,14 @@
     def _():
         greet((seq - 1, me))
 
-    (u0, _, m0, e0), (u1, _, m1, e1) = factors(step_ref, decay_ref)
+    load(0).wait()
+    load(1).wait()
+    (u0, w0, m0, e0), (u1, w1, m1, e1) = factors(step_ref, decay_ref)
     fac[...] = split(
         jnp.concatenate([u0, u1, pad8([jnp.exp(e0 - m0 + e1), jnp.exp(e1 - m1)])], axis=0)
     )
+    aux = [jnp.exp(m0), jnp.exp(m1 + e0), jnp.exp(m1 + e0 - m0), skip_ref[...]]
+    fac_out[...] = split(jnp.concatenate([w0, w1, pad8(aux)], axis=0))
     tot[me] = jnp.broadcast_to(e0 + e1, (8, heads))
 
     @pl.when(first)
@@ -227,15 +278,19 @@
         k, i = t // ways, lax.rem(t, ways)
         q = lax.rem(me + 1 + i, ways)
         index = q * depth + k
-        columns = pl.ds(pl.multiple_of(index * PIECE, PIECE), PIECE)
+        columns = columns_of(index)
         group = index * PIECE // (width // GROUPS)
         shared = pl.ds(pl.multiple_of(group * STATE, STATE), STATE)
+        load_x(index).wait()
         wide = dot(fac[...], spread(index, heads, PIECE))
         state = None
         for c in range(2):
             rows = slice(c * CHUNK, (c + 1) * CHUNK)
             drive = (wide[rows] * x_ref[rows, columns].astype(F32)).astype(BF16)
+            drive_ref[rows, columns] = drive
             part = dot_rows(inject_ref[rows, shared], drive)
+            if c == 0:
+                first_state[index] = part
             part = part * wide[2 * CHUNK + c : 2 * CHUNK + c + 1]
             state = part if state is None else state + part
 
@@ -250,6 +305,7 @@
 
         return carry
 
+    load(2).wait()
     lax.fori_loop(0, depth * ways, piece, 0)
 
     for i in range(1, ways):
@@ -335,13 +391,65 @@
 
         lax.fori_loop(0, depth, finish, 0)
 
+    load(3).wait()
+    mask = lower(CHUNK)
+
+    def prepare(index, carry):
+        columns = columns_of(index)
+        after_ref[:, columns] = dot(fac_out[...], spread(index, heads, PIECE))
+        return carry
+
+    def cross(group, carry):
+        shared = pl.ds(pl.multiple_of(group * STATE, STATE), STATE)
+        for c in range(2):
+            rows = slice(c * CHUNK, (c + 1) * CHUNK)
+            readout = readout_ref[rows, shared]
+            both = dot_last(readout, inject_ref[rows, shared])
+            left_ref[group, rows, :CHUNK] = jnp.where(mask, both, 0.0).astype(BF16)
+            left_ref[group, rows, CHUNK:] = readout
+        return carry
+
+    lax.fori_loop(0, GROUPS, cross, 0)
+    lax.fori_loop(0, width // PIECE, prepare, 0)
+
+    def result(k, q):
+        index = q * depth + k
+        columns = columns_of(index)
+        group = index * PIECE // (width // GROUPS)
+        held = held_ref[index].astype(F32)
+        rest = after_ref[2 * CHUNK : 2 * CHUNK + 8, columns]
+        enter = held * rest[0:1]
+        for c in range(2):
+            rows = slice(c * CHUNK, (c + 1) * CHUNK)
+            right = jnp.concatenate([drive_ref[rows, columns], enter.astype(BF16)], axis=0)
+            acc = dot(left_ref[group, rows, :], right)
+            plain = rest[3:4] * x_ref[rows, columns].astype(F32)
+            x_ref[rows, columns] = (after_ref[rows, columns] * acc + plain).astype(BF16)
+            if c == 0:
+                enter = held * rest[1:2] + first_state[index] * rest[2:3]
+        store(index).start()
+
+    def results(t, carry):
+        k, i = t // ways, lax.rem(t, ways)
+        q = lax.rem(me + i, ways)
+
+        @pl.when(i == 0)
+        def _():
+            keep_copy(k).wait()
+
+        @pl.when(i > 0)
+        def _():
+            down_from(k, q).wait_recv()
+
+        result(k, q)
+        return carry
+
+    lax.fori_loop(0, depth * ways, results, 0)
+
     def drain(k, carry):
-        for i in range(1, ways):
-            down_from(k, other(i)).wait_recv()
         for i in range(1, ways):
             up_copy(k, other(i)).wait_send()
             down_copy(k, other(i)).wait_send()
-        keep_copy(k).wait()
 
         @pl.when(core == 0)
         def _():
@@ -355,61 +463,45 @@
         return carry
 
     lax.fori_loop(0, depth, drain, 0)
+
+    def stored(index, carry):
+        store(index).wait()
+        return carry
+
+    lax.fori_loop(0, width // PIECE, stored, 0)
     for i in range(1, ways):
         tot_copy(other(i)).wait_send()
 
     @pl.when(core == 0)
     def _():
         pair_copy().wait_send()
-
-
-def output_kernel(
-    x_ref, step_ref, decay_ref, inject_ref, readout_ref, skip_ref, held_ref, out_ref, fac
-):
-    heads = step_ref.shape[1]
-    group = pl.program_id(0)
-
-    @pl.when(group == 0)
-    def _():
-        (u0, w0, m0, e0), (u1, w1, m1, e1) = factors(step_ref, decay_ref)
-        aux = [jnp.exp(m0), jnp.exp(m1 + e0), jnp.exp(m1 + e0 - m0), skip_ref[...]]
-        fac[...] = split(jnp.concatenate([u0, u1, w0, w1, pad8(aux)], axis=0))
-
-    wide = dot(fac[...], spread(group, heads, x_ref.shape[1]))
-    aux = 4 * CHUNK
-    held = jnp.concatenate([held_ref[i] for i in range(held_ref.shape[0])], axis=1).astype(F32)
-    mask = lower(CHUNK)
-    enter = held * wide[aux : aux + 1]
-    for c in range(2):
-        rows = slice(c * CHUNK, (c + 1) * CHUNK)
-        x = x_ref[rows, :].astype(F32)
-        drive = (wide[rows] * x).astype(BF16)
-        inject, readout = inject_ref[rows, :], readout_ref[rows, :]
-        cross = jnp.where(mask, dot_last(readout, inject), 0.0).astype(BF16)
-        left = jnp.concatenate([cross, readout], axis=1)
-        right = jnp.concatenate([drive, enter.astype(BF16)], axis=0)
-        acc = dot(left, right)
-        after = wide[(2 + c) * CHUNK : (3 + c) * CHUNK]
-        out_ref[rows, :] = (after * acc + wide[aux + 3 : aux + 4] * x).astype(BF16)
-        if c == 0:
-            enter = held * wide[aux + 1 : aux + 2] + dot_rows(inject, drive) * wide[aux + 2 : aux + 3]
 
 
 def shards(features, step_size, log_decay, inject, readout, skip_gain):
     ways, seqs = lax.axis_size("head"), lax.axis_size("seq")
     tokens, width = features.shape
     heads = step_size.shape[1]
-    block = width // GROUPS
     depth = width // ways // PIECE
-    params = pltpu.CompilerParams(vmem_limit_bytes=48 * 2**20)
+    pieces = width // PIECE
     vmem = pl.BlockSpec(memory_space=pltpu.VMEM)
     dma = pltpu.SemaphoreType.DMA
-    held = pl.pallas_call(
-        functools.partial(scan_kernel, ways, seqs),
-        in_specs=[vmem] * 4,
+    return pl.pallas_call(
+        functools.partial(mixer_kernel, ways, seqs),
+        in_specs=[pl.BlockSpec(memory_space=pl.ANY)] * 5 + [vmem],
         out_specs=pl.BlockSpec(memory_space=pl.ANY),
-        out_shape=jax.ShapeDtypeStruct((width // PIECE, STATE, PIECE), BF16),
+        out_shape=jax.ShapeDtypeStruct((tokens, width), BF16),
         scratch_shapes=[
+            pltpu.VMEM((tokens, width), BF16),
+            pltpu.VMEM((tokens, heads), F32),
+            pltpu.VMEM((tokens, heads), F32),
+            pltpu.VMEM((tokens, GROUPS * STATE), BF16),
+            pltpu.VMEM((tokens, GROUPS * STATE), BF16),
+            pltpu.VMEM((pieces, STATE, PIECE), BF16),
+            pltpu.VMEM((tokens, width), BF16),
+            pltpu.VMEM((pieces, STATE, PIECE), F32),
+            pltpu.VMEM((tokens + 16, width), F32),
+            pltpu.VMEM((GROUPS, tokens, CHUNK + STATE), BF16),
+            pltpu.VMEM((2 * CHUNK + 16, 2 * heads), BF16),
             pltpu.VMEM((2 * CHUNK + 16, 2 * heads), BF16),
             pltpu.VMEM((ways, 8, heads), F32),
             pltpu.VMEM((2, 8, heads), F32),
@@ -434,26 +526,14 @@
             dma((depth, 2)),
             dma((depth,)),
             dma((depth,)),
+            dma((4,)),
+            dma((pieces,)),
+            dma((pieces,)),
         ],
         compiler_params=pltpu.CompilerParams(
-            vmem_limit_bytes=48 * 2**20, collective_id=0, has_side_effects=True
+            vmem_limit_bytes=60 * 2**20, collective_id=0, has_side_effects=True
         ),
-    )(features, step_size, log_decay, inject)
-
-    wide_spec = pl.BlockSpec((tokens, block), lambda g: (0, g))
-    full = pl.BlockSpec((tokens, heads), lambda g: (0, 0))
-    group_spec = pl.BlockSpec((tokens, STATE), lambda g: (0, g))
-    state_spec = pl.BlockSpec((block // PIECE, STATE, PIECE), lambda g: (g, 0, 0))
-    row_spec = pl.BlockSpec((1, heads), lambda g: (0, 0))
-    return pl.pallas_call(
-        output_kernel,
-        grid=(GROUPS,),
-        in_specs=[wide_spec, full, full, group_spec, group_spec, row_spec, state_spec],
-        out_specs=wide_spec,
-        out_shape=jax.ShapeDtypeStruct((tokens, width), BF16),
-        scratch_shapes=[pltpu.VMEM((4 * CHUNK + 16, 2 * heads), BF16)],
-        compiler_params=params,
-    )(features, step_size, log_decay, inject, readout, skip_gain[None], held)
+    )(features, step_size, log_decay, inject, readout, skip_gain[None])
 
 
 def solution(mesh):

time: 69 us -> 59.4 us (0.86)
  Pallas kernels: 65.7 us -> 54.6 us
  local copies, waits for them, and re-layouts: 2.87 us -> 4.64 us
    pallas_call x2 -> x1, Pallas kernels: 65.7 us -> 54.6 us  [shards(): pl.pallas_call(functools.partial(mixer_kernel, ways, seqs), in_specs=[pl....]
    unnamed x10 -> x1, local copies, waits for them, and re-layouts: 2.87 us -> 4.64 us
where the time goes in v3:
time: 59.4 us; the launch traced here: 59.3 us
  Pallas kernels  54.6 us (92%)
  local copies, waits for them, and re-layouts  4.64 us (8%)
    pallas_call x1, Pallas kernels, shards(): pl.pallas_call(functools.partial(mixer_kernel, ways, seqs), in_specs=[pl....  54.6 us
    unnamed x1, local copies, waits for them, and re-layouts  4.64 us

profile of v3, /device:TPU:0, one launch (start us, length us, event | category | flops | bytes accessed | tf_op | source)
XLA Modules:
  0.0 59.3 jit_solution(5077697393630929394)
XLA Ops:
  0.0 54.6 %shard_map.64 = bf16[256,8192]{1,0:T(8,128)(2,1)} custom-call(bf16[256,8192]{1,0:T(8,128)(2,1)} %x_hbm.1, f32[256,128]{1,0:T(8,128)} %step_hbm.1, f32[256,128]{1,0:T(8,128)} %decay_hbm.1, bf16[256,1024]{1,0:T(8,128)(2,1)} %inject_hbm.1, bf16[256,1024]{1,0:T(8,128)(2,1)} %readout_hbm.1, f32[1,128]{1,0:T(1,128)} %bitcast.1), custom_call_target="tpu_custom_call" | custom-call | tf_op jit(solution)/shard_map/pallas_call | solution.py:488
  54.6 4.6 %copy.8 = bf16[256,8192]{1,0:T(8,128)(2,1)} copy(bf16[256,8192]{1,0:T(8,128)(2,1)} %shard_map.64) | data formatting | bytes 8388608

commit v4 on v3

--- a/solution.py
+++ b/solution.py
@@ -11,7 +11,7 @@
 STATE = 128
 GROUPS = 8
 CHUNK = 128
-PIECE = 512
+PIECE = 256
 MESH = pl.DeviceIdType.MESH
 F32 = jnp.float32
 BF16 = jnp.bfloat16
@@ -82,7 +82,7 @@
     inject_hbm,
     readout_hbm,
     skip_ref,
-    out_hbm,
+    out_ref,
     x_ref,
     step_ref,
     decay_ref,
@@ -120,7 +120,6 @@
     keep_sem,
     load_sem,
     x_sem,
-    out_sem,
 ):
     heads = step_ref.shape[1]
     width = x_ref.shape[1]
@@ -158,12 +157,6 @@
     def load_x(index):
         columns = columns_of(index)
         return pltpu.make_async_copy(x_hbm.at[:, columns], x_ref.at[:, columns], x_sem.at[index])
-
-    def store(index):
-        columns = columns_of(index)
-        return pltpu.make_async_copy(
-            x_ref.at[:, columns], out_hbm.at[:, columns], out_sem.at[index]
-        )
 
     def place(t):
         return lax.rem(me + 1 + lax.rem(t, ways), ways) * depth + t // ways
@@ -360,16 +353,12 @@
                 running = onward(k, running, j)
             total_stage[k] = running.astype(BF16)
             total_copy(k).start()
-            return carry
-
-        def finish(k, carry):
             await_enter(k)
             returns(k, enter_in[k].astype(F32))
             send_down(k)
             return carry
 
         lax.fori_loop(0, depth, totals, 0)
-        lax.fori_loop(0, depth, finish, 0)
 
     @pl.when(core == 1)
     def _():
@@ -424,10 +413,9 @@
             right = jnp.concatenate([drive_ref[rows, columns], enter.astype(BF16)], axis=0)
             acc = dot(left_ref[group, rows, :], right)
             plain = rest[3:4] * x_ref[rows, columns].astype(F32)
-            x_ref[rows, columns] = (after_ref[rows, columns] * acc + plain).astype(BF16)
+            out_ref[rows, columns] = (after_ref[rows, columns] * acc + plain).astype(BF16)
             if c == 0:
                 enter = held * rest[1:2] + first_state[index] * rest[2:3]
-        store(index).start()
 
     def results(t, carry):
         k, i = t // ways, lax.rem(t, ways)
@@ -463,12 +451,6 @@
         return carry
 
     lax.fori_loop(0, depth, drain, 0)
-
-    def stored(index, carry):
-        store(index).wait()
-        return carry
-
-    lax.fori_loop(0, width // PIECE, stored, 0)
     for i in range(1, ways):
         tot_copy(other(i)).wait_send()
 
@@ -487,9 +469,9 @@
     dma = pltpu.SemaphoreType.DMA
     return pl.pallas_call(
         functools.partial(mixer_kernel, ways, seqs),
-        in_specs=[pl.BlockSpec(memory_space=pl.ANY)] * 5 + [vmem],
-        out_specs=pl.BlockSpec(memory_space=pl.ANY),
-        out_shape=jax.ShapeDtypeStruct((tokens, width), BF16),
+        in_specs=[pl.BlockSpec(memory_space=pltpu.HBM)] * 5 + [vmem],
+        out_specs=vmem,
+        out_shape=pltpu.VMEM((tokens, width), BF16),
         scratch_shapes=[
             pltpu.VMEM((tokens, width), BF16),
             pltpu.VMEM((tokens, heads), F32),
@@ -528,10 +510,9 @@
             dma((depth,)),
             dma((4,)),
             dma((pieces,)),
-            dma((pieces,)),
         ],
         compiler_params=pltpu.CompilerParams(
-            vmem_limit_bytes=60 * 2**20, collective_id=0, has_side_effects=True
+            vmem_limit_bytes=59 * 2**20, collective_id=0, has_side_effects=True
         ),
     )(features, step_size, log_decay, inject, readout, skip_gain[None])
 

time: 59.4 us -> 57.4 us (0.966)
  local copies, waits for them, and re-layouts: 4.64 us -> 2.02 us
    unnamed x1, local copies, waits for them, and re-layouts: 4.64 us -> 2.02 us
where the time goes in v4:
time: 57.4 us; the launch traced here: 57 us
  Pallas kernels  54.9 us (96%)
  local copies, waits for them, and re-layouts  2.02 us (4%)
    pallas_call x1, Pallas kernels, shards(): pl.pallas_call(functools.partial(mixer_kernel, ways, seqs), in_specs=[pl....  54.9 us
    unnamed x1, local copies, waits for them, and re-layouts  2.02 us

profile of v4, /device:TPU:0, one launch (start us, length us, event | category | flops | bytes accessed | tf_op | source)
XLA Modules:
  0.0 57.0 jit_solution(6730019179759620101)
XLA Ops:
  0.0 54.9 %shard_map.64 = bf16[256,8192]{1,0:T(8,128)(2,1)S(1)} custom-call(bf16[256,8192]{1,0:T(8,128)(2,1)} %x_hbm.1, f32[256,128]{1,0:T(8,128)} %step_hbm.1, f32[256,128]{1,0:T(8,128)} %decay_hbm.1, bf16[256,1024]{1,0:T(8,128)(2,1)} %inject_hbm.1, bf16[256,1024]{1,0:T(8,128)(2,1)} %readout_hbm.1, f32[1,128]{1,0:T(1,128)} %bitcast.1), custom_call_target="tpu_custom_call" | custom-call | tf_op jit(solution)/shard_map/pallas_call | solution.py:470
  55.0 2.0 %copy.8 = bf16[256,8192]{1,0:T(8,128)(2,1)} copy(bf16[256,8192]{1,0:T(8,128)(2,1)S(1)} %shard_map.64) | data formatting | bytes 8388608

commit v5 on v4

--- a/solution.py
+++ b/solution.py
@@ -73,62 +73,35 @@
     return jnp.concatenate(rows + [jnp.zeros_like(rows[0])] * (16 - len(rows)), axis=0)
 
 
-def mixer_kernel(
-    ways,
-    seqs,
-    x_hbm,
-    step_hbm,
-    decay_hbm,
-    inject_hbm,
-    readout_hbm,
-    skip_ref,
-    out_ref,
-    x_ref,
-    step_ref,
-    decay_ref,
-    inject_ref,
-    readout_ref,
-    held_ref,
-    drive_ref,
-    first_state,
-    after_ref,
-    left_ref,
-    fac,
-    fac_out,
-    tot,
-    pair,
-    dec,
-    up_stage,
-    parts,
-    down_stage,
-    total_stage,
-    total_in,
-    next_stage,
-    enter_in,
-    tot_send,
-    tot_recv,
-    pair_send,
-    pair_recv,
-    up_send,
-    up_recv,
-    down_send,
-    down_recv,
-    total_send,
-    total_recv,
-    next_send,
-    enter_recv,
-    keep_sem,
-    load_sem,
-    x_sem,
-):
+def mixer_kernel(ways, seqs, *refs):
+    levels = ways.bit_length() - 1
+    refs = list(refs)
+
+    def take(count):
+        out = refs[:count]
+        del refs[:count]
+        return out
+
+    x_hbm, step_hbm, decay_hbm, inject_hbm, readout_hbm, skip_ref, out_ref = take(7)
+    x_ref, step_ref, decay_ref, inject_ref, readout_ref = take(5)
+    drive_ref, first_state, after_ref, left_ref, fac, fac_out, tot, pair, dec = take(9)
+    level_total, level_in, down_stage = take(levels), take(levels), take(levels)
+    enter_at = take(levels + 1)
+    top_total, total_in, next_stage, enter_in = take(4)
+    tot_send, tot_recv, pair_send, pair_recv, up_send, up_recv, down_send, down_recv = take(8)
+    total_send, total_recv, next_send, enter_recv, load_sem, x_sem = take(6)
     heads = step_ref.shape[1]
     width = x_ref.shape[1]
-    own = width // ways
-    depth = own // PIECE
+    depth = width // ways // PIECE
     me, seq = lax.axis_index("head"), lax.axis_index("seq")
     core, chip = lax.rem(seq, 2), seq // 2
     chips = seqs // 2
-    first = chip == 0
+    bits = [lax.rem(me // 2**l, 2) for l in range(levels)]
+    mates = [me + 2**l * (1 - 2 * bits[l]) for l in range(levels)]
+    count = [ways // 2**l for l in range(levels + 1)]
+    starts = [0]
+    for l in range(levels):
+        starts.append(starts[l] + bits[l] * count[l + 1])
 
     def peer(q):
         return (seq, q)
@@ -158,14 +131,14 @@
         columns = columns_of(index)
         return pltpu.make_async_copy(x_hbm.at[:, columns], x_ref.at[:, columns], x_sem.at[index])
 
-    def place(t):
-        return lax.rem(me + 1 + lax.rem(t, ways), ways) * depth + t // ways
+    def owner(i):
+        return lax.rem(i + (1 - bits[0]) * count[1], ways)
 
     for i in range(3):
         load(i).start()
 
     def begin(t, carry):
-        load_x(place(t)).start()
+        load_x(owner(lax.rem(t, ways)) * depth + t // ways).start()
         return carry
 
     lax.fori_loop(0, depth * ways, begin, 0)
@@ -201,7 +174,7 @@
     fac_out[...] = split(jnp.concatenate([w0, w1, pad8(aux)], axis=0))
     tot[me] = jnp.broadcast_to(e0 + e1, (8, heads))
 
-    @pl.when(first)
+    @pl.when(chip == 0)
     def _():
         enter_in[...] = jnp.zeros_like(enter_in)
 
@@ -214,37 +187,34 @@
     def tot_from(q):
         return remote(tot.at[q], tot.at[q], tot_send.at[q], tot_recv.at[q], peer(q))
 
-    def up_copy(k, q):
+    def up_copy(l, k):
+        half = count[l + 1]
         return remote(
-            up_stage.at[k, q], parts.at[k, me], up_send.at[k, q], up_recv.at[k, me], peer(q)
+            level_total[l].at[pl.ds(k * count[l] + (1 - bits[l]) * half, half)],
+            level_in[l].at[pl.ds(k * half, half)],
+            up_send.at[l, k],
+            up_recv.at[l, k],
+            peer(mates[l]),
         )
 
-    def up_from(k, q):
+    def down_copy(l, k):
+        half = count[l + 1]
         return remote(
-            up_stage.at[k, q], parts.at[k, q], up_send.at[k, q], up_recv.at[k, q], peer(q)
+            down_stage[l].at[pl.ds(k * half, half)],
+            enter_at[l].at[pl.ds(k * count[l] + bits[l] * half, half)],
+            down_send.at[l, k],
+            down_recv.at[l, k],
+            peer(mates[l]),
         )
 
-    def down_copy(k, q):
+    def down_from(l, k):
+        half = count[l + 1]
         return remote(
-            down_stage.at[k, q],
-            held_ref.at[me * depth + k],
-            down_send.at[k, q],
-            down_recv.at[k, me],
-            peer(q),
-        )
-
-    def down_from(k, q):
-        return remote(
-            down_stage.at[k, q],
-            held_ref.at[q * depth + k],
-            down_send.at[k, q],
-            down_recv.at[k, q],
-            peer(q),
-        )
-
-    def keep_copy(k):
-        return pltpu.make_async_copy(
-            down_stage.at[k, me], held_ref.at[me * depth + k], keep_sem.at[k]
+            down_stage[l].at[pl.ds(k * half, half)],
+            enter_at[l].at[pl.ds(k * count[l] + (1 - bits[l]) * half, half)],
+            down_send.at[l, k],
+            down_recv.at[l, k],
+            peer(mates[l]),
         )
 
     def pair_copy():
@@ -252,7 +222,7 @@
 
     def total_copy(k):
         return remote(
-            total_stage.at[k], total_in.at[k], total_send.at[k], total_recv.at[k], (seq + 1, me)
+            top_total.at[k], total_in.at[k], total_send.at[k], total_recv.at[k], (seq + 1, me)
         )
 
     def next_copy(k, ahead):
@@ -269,7 +239,7 @@
 
     def piece(t, carry):
         k, i = t // ways, lax.rem(t, ways)
-        q = lax.rem(me + 1 + i, ways)
+        q = owner(i)
         index = q * depth + k
         columns = columns_of(index)
         group = index * PIECE // (width // GROUPS)
@@ -286,15 +256,11 @@
                 first_state[index] = part
             part = part * wide[2 * CHUNK + c : 2 * CHUNK + c + 1]
             state = part if state is None else state + part
-
-        @pl.when(i == ways - 1)
-        def _():
-            parts[k, me] = state.astype(BF16)
-
-        @pl.when(i < ways - 1)
-        def _():
-            up_stage[k, q] = state.astype(BF16)
-            up_copy(k, q).start()
+        level_total[0][k * ways + q] = state.astype(BF16)
+
+        @pl.when(i == count[1] - 1)
+        def _():
+            up_copy(0, k).start()
 
         return carry
 
@@ -303,8 +269,12 @@
 
     for i in range(1, ways):
         tot_from(other(i)).wait_recv()
-    logs = [tot[j][:1] for j in range(ways)]
-    whole = sum(logs[1:], logs[0])
+
+    def log_sum(first, n):
+        rows = [tot[first + i][:1] for i in range(n)]
+        return sum(rows[1:], rows[0])
+
+    whole = log_sum(0, ways)
 
     @pl.when(core == 0)
     def _():
@@ -316,71 +286,84 @@
     def _():
         pair_copy().wait_recv()
 
-    rows = [jnp.exp(a) for a in logs] + [jnp.exp(pair[1][:1])]
-    rows = split(jnp.concatenate(rows + [jnp.zeros_like(rows[0])] * (-len(rows) % 16), axis=0))
-    for k in range(depth):
-        dec[k] = dot(rows, spread(me * depth + k, heads, PIECE))
-
-    def await_parts(k):
-        for i in range(1, ways):
-            up_from(k, other(i)).wait_recv()
-
-    def onward(k, running, j):
-        return running * dec[k, j : j + 1, :] + parts[k, j].astype(F32)
-
-    def returns(k, running):
-        for j in range(ways):
-            down_stage[k, j] = running.astype(BF16)
-            running = onward(k, running, j)
-        return running
-
-    def send_down(k):
-        for i in range(1, ways):
-            down_copy(k, other(i)).start()
-        keep_copy(k).start()
-
-    def await_enter(k):
+    rows = []
+    for l in range(levels):
+        base = me // 2 ** (l + 1) * 2 ** (l + 1)
+        rows += [log_sum(base, 2**l), log_sum(base + 2**l, 2**l)]
+    rows = split(jnp.exp(pad8(rows + [whole, pair[1][:1]])))
+
+    def widen(t, carry):
+        k, i = t // count[1], lax.rem(t, count[1])
+        dec[t] = dot(rows, spread((starts[1] + i) * depth + k, heads, PIECE))
+        return carry
+
+    lax.fori_loop(0, depth * count[1], widen, 0)
+
+    def decay_row(l, k, i, row):
+        at = k * count[1] + starts[l + 1] - starts[1] + i
+        return dec[at][row : row + 1]
+
+    def sides(l, k, i):
+        half = count[l + 1]
+        own = level_total[l][k * count[l] + bits[l] * half + i].astype(F32)
+        came = level_in[l][k * half + i].astype(F32)
+        return jnp.where(bits[l] == 0, own, came), jnp.where(bits[l] == 0, came, own)
+
+    def up(l, k):
+        up_copy(l, k).wait_recv()
+        for i in range(count[l + 1]):
+            left, right = sides(l, k, i)
+            both = (left * decay_row(l, k, i, 2 * l + 1) + right).astype(BF16)
+            if l + 1 < levels:
+                level_total[l + 1][k * count[l + 1] + i] = both
+            else:
+                top_total[k] = both
+        if l + 1 < levels:
+            up_copy(l + 1, k).start()
+        else:
+
+            @pl.when(core == 0)
+            def _():
+                total_copy(k).start()
+
+    def top(k):
         @pl.when(chip > 0)
         def _():
             next_copy(k, 1).wait_recv()
 
-    @pl.when(core == 0)
-    def _():
-        def totals(k, carry):
-            await_parts(k)
-            running = parts[k, 0].astype(F32)
-            for j in range(1, ways):
-                running = onward(k, running, j)
-            total_stage[k] = running.astype(BF16)
-            total_copy(k).start()
-            await_enter(k)
-            returns(k, enter_in[k].astype(F32))
-            send_down(k)
-            return carry
-
-        lax.fori_loop(0, depth, totals, 0)
-
-    @pl.when(core == 1)
-    def _():
-        def finish(k, carry):
-            await_parts(k)
+        @pl.when(core == 0)
+        def _():
+            enter_at[levels][k] = enter_in[k]
+
+        @pl.when(core == 1)
+        def _():
             total_copy(k).wait_recv()
-            await_enter(k)
-            start = enter_in[k].astype(F32) * dec[k, ways : ways + 1, :]
-            running = returns(k, start + total_in[k].astype(F32))
+            start = enter_in[k].astype(F32) * decay_row(levels - 1, k, 0, 2 * levels + 1)
+            start = start + total_in[k].astype(F32)
+            after = start * decay_row(levels - 1, k, 0, 2 * levels) + top_total[k].astype(F32)
 
             @pl.when(chip < chips - 1)
             def _():
-                next_stage[k] = running.astype(BF16)
+                next_stage[k] = after.astype(BF16)
                 next_copy(k, 2).start()
                 next_copy(k, 1).start()
 
-            send_down(k)
-            return carry
-
-        lax.fori_loop(0, depth, finish, 0)
-
-    load(3).wait()
+            enter_at[levels][k] = start.astype(BF16)
+
+    def down(l, k):
+        half = count[l + 1]
+        if l + 1 < levels:
+            down_from(l + 1, k).wait_recv()
+        for i in range(half):
+            enter = enter_at[l + 1][k * half + i].astype(F32)
+            left, _ = sides(l, k, i)
+            later = enter * decay_row(l, k, i, 2 * l) + left
+            mine = jnp.where(bits[l] == 0, enter, later)
+            theirs = jnp.where(bits[l] == 0, later, enter)
+            down_stage[l][k * half + i] = theirs.astype(BF16)
+            enter_at[l][k * count[l] + bits[l] * half + i] = mine.astype(BF16)
+        down_copy(l, k).start()
+
     mask = lower(CHUNK)
 
     def prepare(index, carry):
@@ -398,14 +381,40 @@
             left_ref[group, rows, CHUNK:] = readout
         return carry
 
+    def advance(t, carry):
+        def stage(lag, work):
+            @pl.when((t >= lag) & (t < depth + lag))
+            def _():
+                work(t - lag)
+
+        for l in range(levels):
+            stage(l, functools.partial(up, l))
+        stage(levels, top)
+        for n, l in enumerate(reversed(range(levels))):
+            stage(levels + n, functools.partial(down, l))
+
+        @pl.when(t < depth)
+        def _():
+            lax.fori_loop(t * ways, (t + 1) * ways, prepare, 0)
+
+        return carry
+
+    lax.fori_loop(0, depth + 2 * levels - 1, advance, 0)
+    load(3).wait()
     lax.fori_loop(0, GROUPS, cross, 0)
-    lax.fori_loop(0, width // PIECE, prepare, 0)
-
-    def result(k, q):
+
+    def results(t, carry):
+        k, i = t // ways, lax.rem(t, ways)
+        q = lax.rem(i + bits[0] * count[1], ways)
+
+        @pl.when(i == count[1])
+        def _():
+            down_from(0, k).wait_recv()
+
         index = q * depth + k
         columns = columns_of(index)
         group = index * PIECE // (width // GROUPS)
-        held = held_ref[index].astype(F32)
+        held = enter_at[0][k * ways + q].astype(F32)
         rest = after_ref[2 * CHUNK : 2 * CHUNK + 8, columns]
         enter = held * rest[0:1]
         for c in range(2):
@@ -416,28 +425,14 @@
             out_ref[rows, columns] = (after_ref[rows, columns] * acc + plain).astype(BF16)
             if c == 0:
                 enter = held * rest[1:2] + first_state[index] * rest[2:3]
-
-    def results(t, carry):
-        k, i = t // ways, lax.rem(t, ways)
-        q = lax.rem(me + i, ways)
-
-        @pl.when(i == 0)
-        def _():
-            keep_copy(k).wait()
-
-        @pl.when(i > 0)
-        def _():
-            down_from(k, q).wait_recv()
-
-        result(k, q)
         return carry
 
     lax.fori_loop(0, depth * ways, results, 0)
 
     def drain(k, carry):
-        for i in range(1, ways):
-            up_copy(k, other(i)).wait_send()
-            down_copy(k, other(i)).wait_send()
+        for l in range(levels):
+            up_copy(l, k).wait_send()
+            down_copy(l, k).wait_send()
 
         @pl.when(core == 0)
         def _():
@@ -465,6 +460,11 @@
     heads = step_size.shape[1]
     depth = width // ways // PIECE
     pieces = width // PIECE
+    levels = ways.bit_length() - 1
+
+    def states(count):
+        return pltpu.VMEM((count, STATE, PIECE), BF16)
+
     vmem = pl.BlockSpec(memory_space=pltpu.VMEM)
     dma = pltpu.SemaphoreType.DMA
     return pl.pallas_call(
@@ -478,7 +478,6 @@
             pltpu.VMEM((tokens, heads), F32),
             pltpu.VMEM((tokens, GROUPS * STATE), BF16),
             pltpu.VMEM((tokens, GROUPS * STATE), BF16),
-            pltpu.VMEM((pieces, STATE, PIECE), BF16),
             pltpu.VMEM((tokens, width), BF16),
             pltpu.VMEM((pieces, STATE, PIECE), F32),
             pltpu.VMEM((tokens + 16, width), F32),
@@ -487,26 +486,20 @@
             pltpu.VMEM((2 * CHUNK + 16, 2 * heads), BF16),
             pltpu.VMEM((ways, 8, heads), F32),
             pltpu.VMEM((2, 8, heads), F32),
-            pltpu.VMEM((depth, (ways + 16) // 16 * 16, PIECE), F32),
-            pltpu.VMEM((depth, ways, STATE, PIECE), BF16),
-            pltpu.VMEM((depth, ways, STATE, PIECE), BF16),
-            pltpu.VMEM((depth, ways, STATE, PIECE), BF16),
-            pltpu.VMEM((depth, STATE, PIECE), BF16),
-            pltpu.VMEM((depth, STATE, PIECE), BF16),
-            pltpu.VMEM((depth, STATE, PIECE), BF16),
-            pltpu.VMEM((depth, STATE, PIECE), BF16),
+            pltpu.VMEM((pieces // 2, 16, PIECE), F32),
+            *[states(pieces // 2**l) for l in range(levels)],
+            *[states(pieces // 2 ** (l + 1)) for l in range(levels)],
+            *[states(pieces // 2 ** (l + 1)) for l in range(levels)],
+            *[states(pieces // 2**l) for l in range(levels + 1)],
+            *[states(depth)] * 4,
             dma((ways,)),
             dma((ways,)),
             dma,
             dma,
-            dma((depth, ways)),
-            dma((depth, ways)),
-            dma((depth, ways)),
-            dma((depth, ways)),
+            *[dma((levels, depth))] * 4,
             dma((depth,)),
             dma((depth,)),
             dma((depth, 2)),
-            dma((depth,)),
             dma((depth,)),
             dma((4,)),
             dma((pieces,)),

time: 57.4 us -> 66 us (1.15)
  the two profiles are of different devices: /device:TPU:0 before, /device:TPU:24 now
where the time goes in v5:
time: 66 us; the launch traced here: 65.9 us
  Pallas kernels  63.9 us (97%)
  local copies, waits for them, and re-layouts  2.02 us (3%)
    pallas_call x1, Pallas kernels, shards(): pl.pallas_call(functools.partial(mixer_kernel, ways, seqs), in_specs=[pl....  63.9 us
    unnamed x1, local copies, waits for them, and re-layouts  2.02 us

profile of v5, /device:TPU:24, one launch (start us, length us, event | category | flops | bytes accessed | tf_op | source)
XLA Modules:
  0.0 65.9 jit_solution(7805437861186219936)
XLA Ops:
  0.0 63.9 %shard_map.64 = bf16[256,8192]{1,0:T(8,128)(2,1)S(1)} custom-call(bf16[256,8192]{1,0:T(8,128)(2,1)} %refs_0_.1, f32[256,128]{1,0:T(8,128)} %refs_1_.1, f32[256,128]{1,0:T(8,128)} %refs_2_.1, bf16[256,1024]{1,0:T(8,128)(2,1)} %refs_3_.1, bf16[256,1024]{1,0:T(8,128)(2,1)} %refs_4_.1, f32[1,128]{1,0:T(1,128)} %bitcast.1), custom_call_target="tpu_custom_call" | custom-call | tf_op jit(solution)/shard_map/pallas_call | solution.py:470
  63.9 2.0 %copy.8 = bf16[256,8192]{1,0:T(8,128)(2,1)} copy(bf16[256,8192]{1,0:T(8,128)(2,1)S(1)} %shard_map.64) | data formatting | bytes 8388608

commit v6 on v5

--- a/solution.py
+++ b/solution.py
@@ -381,6 +381,8 @@
             left_ref[group, rows, CHUNK:] = readout
         return carry
 
+    final_lag = max(depth, 2 * levels + chips - 2)
+
     def advance(t, carry):
         def stage(lag, work):
             @pl.when((t >= lag) & (t < depth + lag))
@@ -389,9 +391,10 @@
 
         for l in range(levels):
             stage(l, functools.partial(up, l))
-        stage(levels, top)
-        for n, l in enumerate(reversed(range(levels))):
-            stage(levels + n, functools.partial(down, l))
+        stage(levels + chip, top)
+        for l in reversed(range(1, levels)):
+            stage(levels + chip + levels - 1 - l, functools.partial(down, l))
+        stage(final_lag, functools.partial(down, 0))
 
         @pl.when(t < depth)
         def _():
@@ -399,7 +402,7 @@
 
         return carry
 
-    lax.fori_loop(0, depth + 2 * levels - 1, advance, 0)
+    lax.fori_loop(0, depth + final_lag, advance, 0)
     load(3).wait()
     lax.fori_loop(0, GROUPS, cross, 0)
 

time: 66 us -> 71.3 us (1.080)
  the two profiles are of different devices: /device:TPU:24 before, /device:TPU:0 now
where the time goes in v6:
time: 71.3 us; the launch traced here: 71.2 us
  Pallas kernels  69.2 us (97%)
  local copies, waits for them, and re-layouts  2.02 us (3%)
    pallas_call x1, Pallas kernels, shards(): pl.pallas_call(functools.partial(mixer_kernel, ways, seqs), in_specs=[pl....  69.2 us
    unnamed x1, local copies, waits for them, and re-layouts  2.02 us

profile of v6, /device:TPU:0, one launch (start us, length us, event | category | flops | bytes accessed | tf_op | source)
XLA Modules:
  0.0 71.2 jit_solution(10816046191329990213)
XLA Ops:
  0.0 69.2 %shard_map.64 = bf16[256,8192]{1,0:T(8,128)(2,1)S(1)} custom-call(bf16[256,8192]{1,0:T(8,128)(2,1)} %refs_0_.1, f32[256,128]{1,0:T(8,128)} %refs_1_.1, f32[256,128]{1,0:T(8,128)} %refs_2_.1, bf16[256,1024]{1,0:T(8,128)(2,1)} %refs_3_.1, bf16[256,1024]{1,0:T(8,128)(2,1)} %refs_4_.1, f32[1,128]{1,0:T(1,128)} %bitcast.1), custom_call_target="tpu_custom_call" | custom-call | tf_op jit(solution)/shard_map/pallas_call | solution.py:473
  69.2 2.0 %copy.8 = bf16[256,8192]{1,0:T(8,128)(2,1)} copy(bf16[256,8192]{1,0:T(8,128)(2,1)S(1)} %shard_map.64) | data formatting | bytes 8388608

commit v7 on v4

--- a/solution.py
+++ b/solution.py
@@ -11,7 +11,8 @@
 STATE = 128
 GROUPS = 8
 CHUNK = 128
-PIECE = 256
+PIECE = 512
+BEHIND = 2
 MESH = pl.DeviceIdType.MESH
 F32 = jnp.float32
 BF16 = jnp.bfloat16
@@ -346,19 +347,31 @@
 
     @pl.when(core == 0)
     def _():
-        def totals(k, carry):
+        def totals(k):
             await_parts(k)
             running = parts[k, 0].astype(F32)
             for j in range(1, ways):
                 running = onward(k, running, j)
             total_stage[k] = running.astype(BF16)
             total_copy(k).start()
+
+        def finish(k):
             await_enter(k)
             returns(k, enter_in[k].astype(F32))
             send_down(k)
+
+        def both(t, carry):
+            @pl.when(t < depth)
+            def _():
+                totals(t)
+
+            @pl.when(t >= BEHIND)
+            def _():
+                finish(t - BEHIND)
+
             return carry
 
-        lax.fori_loop(0, depth, totals, 0)
+        lax.fori_loop(0, depth + BEHIND, both, 0)
 
     @pl.when(core == 1)
     def _():

time: 57.4 us -> 56.1 us (0.977)
  Pallas kernels: 54.9 us -> 53.9 us
    pallas_call x1, Pallas kernels: 54.9 us -> 53.9 us  [shards(): pl.pallas_call(functools.partial(mixer_kernel, ways, seqs), in_specs=[pl....]
where the time goes in v7:
time: 56.1 us; the launch traced here: 55.9 us
  Pallas kernels  53.9 us (96%)
  local copies, waits for them, and re-layouts  2.02 us (4%)
    pallas_call x1, Pallas kernels, shards(): pl.pallas_call(functools.partial(mixer_kernel, ways, seqs), in_specs=[pl....  53.9 us
    unnamed x1, local copies, waits for them, and re-layouts  2.02 us

profile of v7, /device:TPU:0, one launch (start us, length us, event | category | flops | bytes accessed | tf_op | source)
XLA Modules:
  0.0 55.9 jit_solution(2533208340737803815)
XLA Ops:
  0.0 53.9 %shard_map.64 = bf16[256,8192]{1,0:T(8,128)(2,1)S(1)} custom-call(bf16[256,8192]{1,0:T(8,128)(2,1)} %x_hbm.1, f32[256,128]{1,0:T(8,128)} %step_hbm.1, f32[256,128]{1,0:T(8,128)} %decay_hbm.1, bf16[256,1024]{1,0:T(8,128)(2,1)} %inject_hbm.1, bf16[256,1024]{1,0:T(8,128)(2,1)} %readout_hbm.1, f32[1,128]{1,0:T(1,128)} %bitcast.1), custom_call_target="tpu_custom_call" | custom-call | tf_op jit(solution)/shard_map/pallas_call | solution.py:483
  53.9 2.0 %copy.8 = bf16[256,8192]{1,0:T(8,128)(2,1)} copy(bf16[256,8192]{1,0:T(8,128)(2,1)S(1)} %shard_map.64) | data formatting | bytes 8388608

commit v8 on v7

--- a/solution.py
+++ b/solution.py
@@ -13,6 +13,7 @@
 CHUNK = 128
 PIECE = 512
 BEHIND = 2
+STORES = 8
 MESH = pl.DeviceIdType.MESH
 F32 = jnp.float32
 BF16 = jnp.bfloat16
@@ -162,6 +163,26 @@
     def place(t):
         return lax.rem(me + 1 + lax.rem(t, ways), ways) * depth + t // ways
 
+    barrier = pltpu.get_barrier_semaphore()
+
+    def greet(device):
+        pl.semaphore_signal(barrier, inc=1, device_id=device, device_id_type=MESH)
+
+    for i in range(1, ways):
+        greet(peer(other(i)))
+
+    @pl.when(core == 1)
+    def _():
+        greet((seq - 1, me))
+
+    @pl.when((core == 1) & (chip > 0))
+    def _():
+        greet((seq - 2, me))
+
+    @pl.when((core == 0) & (chip > 0))
+    def _():
+        greet((seq - 1, me))
+
     for i in range(3):
         load(i).start()
 
@@ -171,26 +192,6 @@
 
     lax.fori_loop(0, depth * ways, begin, 0)
     load(3).start()
-
-    barrier = pltpu.get_barrier_semaphore()
-
-    def greet(device):
-        pl.semaphore_signal(barrier, inc=1, device_id=device, device_id_type=MESH)
-
-    for i in range(1, ways):
-        greet(peer(other(i)))
-
-    @pl.when(core == 1)
-    def _():
-        greet((seq - 1, me))
-
-    @pl.when((core == 1) & (chip > 0))
-    def _():
-        greet((seq - 2, me))
-
-    @pl.when((core == 0) & (chip > 0))
-    def _():
-        greet((seq - 1, me))
 
     load(0).wait()
     load(1).wait()
@@ -438,19 +439,21 @@
         def _():
             keep_copy(k).wait()
 
+            @pl.when(k > 0)
+            def _():
+                for j in range(1, ways):
+                    down_copy(k - 1, other(j)).wait_send()
+
         @pl.when(i > 0)
         def _():
             down_from(k, q).wait_recv()
 
         result(k, q)
         return carry
-
-    lax.fori_loop(0, depth * ways, results, 0)
 
     def drain(k, carry):
         for i in range(1, ways):
             up_copy(k, other(i)).wait_send()
-            down_copy(k, other(i)).wait_send()
 
         @pl.when(core == 0)
         def _():
@@ -470,6 +473,23 @@
     @pl.when(core == 0)
     def _():
         pair_copy().wait_send()
+
+    lax.fori_loop(0, depth * ways, results, 0)
+
+    for i in range(1, ways):
+        down_copy(depth - 1, other(i)).wait_send()
+
+
+def store_kernel(mixed_ref, out_hbm, sem):
+    rows = mixed_ref.shape[0] // STORES
+    copies = []
+    for i in range(STORES):
+        part = pl.ds(i * rows, rows)
+        copies.append(pltpu.make_async_copy(mixed_ref.at[part], out_hbm.at[part], sem.at[i]))
+    for copy in copies:
+        copy.start()
+    for copy in copies:
+        copy.wait()
 
 
 def shards(features, step_size, log_decay, inject, readout, skip_gain):
@@ -480,7 +500,7 @@
     pieces = width // PIECE
     vmem = pl.BlockSpec(memory_space=pltpu.VMEM)
     dma = pltpu.SemaphoreType.DMA
-    return pl.pallas_call(
+    mixed = pl.pallas_call(
         functools.partial(mixer_kernel, ways, seqs),
         in_specs=[pl.BlockSpec(memory_space=pltpu.HBM)] * 5 + [vmem],
         out_specs=vmem,
@@ -528,6 +548,13 @@
             vmem_limit_bytes=59 * 2**20, collective_id=0, has_side_effects=True
         ),
     )(features, step_size, log_decay, inject, readout, skip_gain[None])
+    return pl.pallas_call(
+        store_kernel,
+        in_specs=[vmem],
+        out_specs=pl.BlockSpec(memory_space=pltpu.HBM),
+        out_shape=jax.ShapeDtypeStruct((tokens, width), BF16),
+        scratch_shapes=[dma((STORES,))],
+    )(mixed)
 
 
 def solution(mesh):

time: 56.1 us -> 60.1 us (1.071)
  Pallas kernels: 53.9 us -> 58 us
    pallas_call x0 -> x1, Pallas kernels: none -> 4.25 us  [shards(): pl.pallas_call(store_kernel, in_specs=[vmem], out_specs=pl.BlockSpec(memo...]
    unnamed x1 -> x2, local copies, waits for them, and re-layouts: 2.02 us -> 1.93 us
where the time goes in v8:
time: 60.1 us; the launch traced here: 60 us
  Pallas kernels  58 us (97%)
  local copies, waits for them, and re-layouts  1.93 us (3%)
    pallas_call x1, Pallas kernels, shards(): pl.pallas_call(functools.partial(mixer_kernel, ways, seqs), in_specs=[pl....  53.8 us
    pallas_call x1, Pallas kernels, shards(): pl.pallas_call(store_kernel, in_specs=[vmem], out_specs=pl.BlockSpec(memo...  4.25 us
    unnamed x2, local copies, waits for them, and re-layouts  1.93 us

profile of v8, /device:TPU:0, one launch (start us, length us, event | category | flops | bytes accessed | tf_op | source)
XLA Modules:
  0.0 60.0 jit_solution(15772750404942429451)
XLA Ops:
  0.0 53.8 %shard_map.64.mixed_ref = bf16[256,8192]{1,0:T(8,128)(2,1)S(1)} custom-call(bf16[256,8192]{1,0:T(8,128)(2,1)} %x_hbm.1, f32[256,128]{1,0:T(8,128)} %step_hbm.1, f32[256,128]{1,0:T(8,128)} %decay_hbm.1, bf16[256,1024]{1,0:T(8,128)(2,1)} %inject_hbm.1, bf16[256,1024]{1,0:T(8,128)(2,1)} %readout_hbm.1, f32[1,128]{1,0:T(1,128)} %bitcast.1), custom_call_target="tpu_custom_call" | custom-call | tf_op jit(solution)/shard_map/pallas_call | solution.py:503
  53.8 0.0 copy-start
  53.8 1.9 %copy-done = bf16[256,8192]{1,0:T(8,128)(2,1)} copy-done((bf16[256,8192]{1,0:T(8,128)(2,1)}, bf16[256,8192]{1,0:T(8,128)(2,1)S(1)}, u32[]{:S(2)}) %copy-start) | copy-done | bytes 4194328
  55.7 4.3 %shard_map.65 = bf16[256,8192]{1,0:T(8,128)(2,1)} custom-call(bf16[256,8192]{1,0:T(8,128)(2,1)} %copy-done), custom_call_target="tpu_custom_call" | custom-call | tf_op jit(solution)/shard_map/pallas_call | solution.py:551
Async XLA Ops:
  53.8 1.9 %copy-start = (bf16[256,8192]{1,0:T(8,128)(2,1)}, bf16[256,8192]{1,0:T(8,128)(2,1)S(1)}, u32[]{:S(2)}) copy-start(bf16[256,8192]{1,0:T(8,128)(2,1)S(1)} %shard_map.64.mixed_ref) | copy-start | bytes 12582916

commit v9 on v8

--- a/solution.py
+++ b/solution.py
@@ -13,7 +13,6 @@
 CHUNK = 128
 PIECE = 512
 BEHIND = 2
-STORES = 8
 MESH = pl.DeviceIdType.MESH
 F32 = jnp.float32
 BF16 = jnp.bfloat16
@@ -207,9 +206,6 @@
     def _():
         enter_in[...] = jnp.zeros_like(enter_in)
 
-    ahead = 2 - 2 * (chip // (chips - 1)) if chips > 1 else 0
-    pl.semaphore_wait(barrier, ways - core + core * ahead)
-
     def tot_copy(q):
         return remote(tot.at[me], tot.at[me], tot_send.at[q], tot_recv.at[me], peer(q))
 
@@ -266,10 +262,7 @@
             (seq + ahead, me),
         )
 
-    for i in range(1, ways):
-        tot_copy(other(i)).start()
-
-    def piece(t, carry):
+    def piece(t):
         k, i = t // ways, lax.rem(t, ways)
         q = lax.rem(me + 1 + i, ways)
         index = q * depth + k
@@ -296,12 +289,29 @@
         @pl.when(i < ways - 1)
         def _():
             up_stage[k, q] = state.astype(BF16)
-            up_copy(k, q).start()
-
+
+    def pass_on(t):
+        k, i = t // ways, lax.rem(t, ways)
+
+        @pl.when(i < ways - 1)
+        def _():
+            up_copy(k, lax.rem(me + 1 + i, ways)).start()
+
+    def step(t, carry):
+        piece(t)
+        pass_on(t)
         return carry
 
     load(2).wait()
-    lax.fori_loop(0, depth * ways, piece, 0)
+    piece(0)
+    ahead = 2 - 2 * (chip // (chips - 1)) if chips > 1 else 0
+    pl.semaphore_wait(barrier, ways - core + core * ahead)
+
+    pass_on(0)
+    for i in range(1, ways):
+        tot_copy(other(i)).start()
+
+    lax.fori_loop(1, depth * ways, step, 0)
 
     for i in range(1, ways):
         tot_from(other(i)).wait_recv()
@@ -480,18 +490,6 @@
         down_copy(depth - 1, other(i)).wait_send()
 
 
-def store_kernel(mixed_ref, out_hbm, sem):
-    rows = mixed_ref.shape[0] // STORES
-    copies = []
-    for i in range(STORES):
-        part = pl.ds(i * rows, rows)
-        copies.append(pltpu.make_async_copy(mixed_ref.at[part], out_hbm.at[part], sem.at[i]))
-    for copy in copies:
-        copy.start()
-    for copy in copies:
-        copy.wait()
-
-
 def shards(features, step_size, log_decay, inject, readout, skip_gain):
     ways, seqs = lax.axis_size("head"), lax.axis_size("seq")
     tokens, width = features.shape
@@ -500,7 +498,7 @@
     pieces = width // PIECE
     vmem = pl.BlockSpec(memory_space=pltpu.VMEM)
     dma = pltpu.SemaphoreType.DMA
-    mixed = pl.pallas_call(
+    return pl.pallas_call(
         functools.partial(mixer_kernel, ways, seqs),
         in_specs=[pl.BlockSpec(memory_space=pltpu.HBM)] * 5 + [vmem],
         out_specs=vmem,
@@ -548,13 +546,6 @@
             vmem_limit_bytes=59 * 2**20, collective_id=0, has_side_effects=True
         ),
     )(features, step_size, log_decay, inject, readout, skip_gain[None])
-    return pl.pallas_call(
-        store_kernel,
-        in_specs=[vmem],
-        out_specs=pl.BlockSpec(memory_space=pltpu.HBM),
-        out_shape=jax.ShapeDtypeStruct((tokens, width), BF16),
-        scratch_shapes=[dma((STORES,))],
-    )(mixed)
 
 
 def solution(mesh):

time: 60.1 us -> 55.6 us (0.925)
  Pallas kernels: 58 us -> 53.4 us
    pallas_call x1 -> x0, Pallas kernels: 4.25 us -> none  [shards(): pl.pallas_call(store_kernel, in_specs=[vmem], out_specs=pl.BlockSpec(memo...]
    unnamed x2 -> x1, local copies, waits for them, and re-layouts: 1.93 us -> 2.02 us
where the time goes in v9:
time: 55.6 us; the launch traced here: 55.5 us
  Pallas kernels  53.4 us (96%)
  local copies, waits for them, and re-layouts  2.02 us (4%)
    pallas_call x1, Pallas kernels, shards(): pl.pallas_call(functools.partial(mixer_kernel, ways, seqs), in_specs=[pl....  53.4 us
    unnamed x1, local copies, waits for them, and re-layouts  2.02 us

profile of v9, /device:TPU:0, one launch (start us, length us, event | category | flops | bytes accessed | tf_op | source)
XLA Modules:
  0.0 55.5 jit_solution(14520043779099758356)
XLA Ops:
  0.0 53.4 %shard_map.64 = bf16[256,8192]{1,0:T(8,128)(2,1)S(1)} custom-call(bf16[256,8192]{1,0:T(8,128)(2,1)} %x_hbm.1, f32[256,128]{1,0:T(8,128)} %step_hbm.1, f32[256,128]{1,0:T(8,128)} %decay_hbm.1, bf16[256,1024]{1,0:T(8,128)(2,1)} %inject_hbm.1, bf16[256,1024]{1,0:T(8,128)(2,1)} %readout_hbm.1, f32[1,128]{1,0:T(1,128)} %bitcast.1), custom_call_target="tpu_custom_call" | custom-call | tf_op jit(solution)/shard_map/pallas_call | solution.py:501
  53.5 2.0 %copy.8 = bf16[256,8192]{1,0:T(8,128)(2,1)} copy(bf16[256,8192]{1,0:T(8,128)(2,1)S(1)} %shard_map.64) | data formatting | bytes 8388608

commit v10 on v9

--- a/solution.py
+++ b/solution.py
@@ -12,7 +12,7 @@
 GROUPS = 8
 CHUNK = 128
 PIECE = 512
-BEHIND = 2
+BEHIND = 1
 MESH = pl.DeviceIdType.MESH
 F32 = jnp.float32
 BF16 = jnp.bfloat16

time: 55.6 us -> 55.6 us (level)
  no operation moved by 1% of the time
where the time goes in v10:
time: 55.6 us; the launch traced here: 55.5 us
  Pallas kernels  53.4 us (96%)
  local copies, waits for them, and re-layouts  2.02 us (4%)
    pallas_call x1, Pallas kernels, shards(): pl.pallas_call(functools.partial(mixer_kernel, ways, seqs), in_specs=[pl....  53.4 us
    unnamed x1, local copies, waits for them, and re-layouts  2.02 us

profile of v10, /device:TPU:0, one launch (start us, length us, event | category | flops | bytes accessed | tf_op | source)
XLA Modules:
  0.0 55.5 jit_solution(10892490706329955164)
XLA Ops:
  0.0 53.4 %shard_map.64 = bf16[256,8192]{1,0:T(8,128)(2,1)S(1)} custom-call(bf16[256,8192]{1,0:T(8,128)(2,1)} %x_hbm.1, f32[256,128]{1,0:T(8,128)} %step_hbm.1, f32[256,128]{1,0:T(8,128)} %decay_hbm.1, bf16[256,1024]{1,0:T(8,128)(2,1)} %inject_hbm.1, bf16[256,1024]{1,0:T(8,128)(2,1)} %readout_hbm.1, f32[1,128]{1,0:T(1,128)} %bitcast.1), custom_call_target="tpu_custom_call" | custom-call | tf_op jit(solution)/shard_map/pallas_call | solution.py:501
  53.5 2.0 %copy.8 = bf16[256,8192]{1,0:T(8,128)(2,1)} copy(bf16[256,8192]{1,0:T(8,128)(2,1)S(1)} %shard_map.64) | data formatting | bytes 8388608
